TPU v7x, 256 devices: a whole 4x4x8 slice. The times are simulated.
256 devices in a mesh: dp: 32 (over z, y), tensor: 8 (over x, core).
Axes of the slice: x: 4, y: 4, z: 8, core: 2. Of those that a mesh axis runs over, the one named last changes fastest.
Arguments:
- queries: bfloat16 [16384, 4096], P('dp', 'tensor'), may hold values from -20 to 20
- cotangent: bfloat16 [16384, 4096], P('dp', 'tensor'), may hold values from -6 to 6
- table: bfloat16 [512, 128, 896], P('dp'), may hold values from -6 to 6
- key_weight: bfloat16 [896, 4096], P(None, 'tensor'), may hold values from -0.1875 to 0.1875
- value_weight: bfloat16 [896, 4096], P(None, 'tensor'), may hold values from -0.1875 to 0.1875
- owners: int32 [256, 2], P('dp'), may hold values from 0 to 31, all different within a row; in each aligned block of 8 rows (0 to 7, 8 to 15, ...) at most 2 rows name the same one
- slots: int32 [256, 2], P('dp'), may hold values from 0 to 15
Outputs:
- attended: bfloat16 [16384, 4096], P('dp', 'tensor')
- d_query: bfloat16 [16384, 4096], P('dp', 'tensor')
- d_table: float32 [512, 128, 896], P('dp', 'tensor')
Inputs may be any that keep to these rules, and one draw needn't show every extreme that they name: `owners`: in each aligned block of 8 rows (the spans of one dp index) no value occurs more than 2 times, and in some block one value occurs exactly 2 times; the two entries of a row differ.
All inputs are finite; a program needn't handle non-finite values.
Results may differ from a plain program's by a relative error of at most 0.0055.
The roundings to bfloat16 on the way count: a program that leaves them out, or rounds other values in their place, can miss the bound.
Values may be sent and summed in bfloat16 or wider, within the bound.
A program may use at most 128 MiB of HBM per device.

v0:
```python
import math

import jax
import jax.numpy as jnp
from jax import lax
from jax.sharding import PartitionSpec as P

HD = 128
SPAN = 64


def on_device(queries, cotangent, table, key_weight, value_weight, owners, slots):
    n_dp = lax.axis_size("dp")
    n_tp = lax.axis_size("tensor")
    spans = owners.shape[0]
    n_requests = 2 * spans
    n_slabs, n_tokens, enc_width = table.shape
    kv_width = key_weight.shape[1]
    n_heads = kv_width // HD
    capacity = max(2, (4 * spans + n_dp - 1) // n_dp)
    tok_share = n_tokens // n_tp
    score_scale = 1.0 / math.sqrt(HD)
    owner_flat = owners.reshape(n_requests)
    slot_flat = slots.reshape(n_requests)
    onehot = (owner_flat[:, None] == jnp.arange(n_dp, dtype=jnp.int32)[None, :]).astype(jnp.int32)
    within = jnp.sum((jnp.cumsum(onehot, axis=0) - onehot) * onehot, axis=1)
    position = owner_flat * capacity + within
    request_buffer = jnp.full((n_dp * capacity,), -1, jnp.int32).at[position].set(slot_flat)
    asked = lax.all_to_all(
        request_buffer.reshape(n_dp, capacity), "dp", split_axis=0, concat_axis=0, tiled=True
    )
    safe_slot = jnp.maximum(asked, 0)
    w_kv = jnp.concatenate([key_weight, value_weight], axis=1)
    sent_rows = table[safe_slot]
    arrived = lax.all_to_all(sent_rows, "dp", split_axis=0, concat_axis=0, tiled=True)
    own_rows = arrived.reshape(n_dp * capacity, n_tokens, enc_width)[position]
    key_value = jnp.dot(own_rows.reshape(-1, enc_width), w_kv, preferred_element_type=jnp.float32)
    key_value = key_value.astype(jnp.bfloat16).reshape(n_requests, n_tokens, 2 * kv_width)
    key_value = key_value.reshape(spans, 2 * n_tokens, 2 * kv_width)
    keys = key_value[:, :, :kv_width].reshape(spans, 2 * n_tokens, n_heads, HD)
    values = key_value[:, :, kv_width:].reshape(spans, 2 * n_tokens, n_heads, HD)
    query_heads = queries.reshape(spans, SPAN, n_heads, HD)
    grad_heads = cotangent.reshape(spans, SPAN, n_heads, HD)
    scores = (
        jnp.einsum("cqhd,ckhd->chqk", query_heads, keys, preferred_element_type=jnp.float32)
        * score_scale
    )
    attn_probs = jax.nn.softmax(scores, axis=-1)
    weights = attn_probs.astype(jnp.bfloat16)
    attended = jnp.einsum("chqk,ckhd->cqhd", weights, values, preferred_element_type=jnp.float32)
    attended = attended.astype(jnp.bfloat16).reshape(spans * SPAN, kv_width)
    d_weights = jnp.einsum(
        "cqhd,ckhd->chqk", grad_heads, values, preferred_element_type=jnp.float32
    )
    row_sums = jnp.sum(d_weights * attn_probs, axis=-1, keepdims=True)
    dscores = (attn_probs * (d_weights - row_sums) * score_scale).astype(jnp.bfloat16)
    d_query = jnp.einsum("chqk,ckhd->cqhd", dscores, keys, preferred_element_type=jnp.float32)
    d_query = d_query.astype(jnp.bfloat16).reshape(spans * SPAN, kv_width)
    d_keys = jnp.einsum(
        "chqk,cqhd->ckhd", dscores, query_heads, preferred_element_type=jnp.float32
    ).astype(jnp.bfloat16)
    d_values = jnp.einsum(
        "chqk,cqhd->ckhd", weights, grad_heads, preferred_element_type=jnp.float32
    ).astype(jnp.bfloat16)
    d_kv = jnp.concatenate(
        [
            d_keys.reshape(spans, 2 * n_tokens, kv_width),
            d_values.reshape(spans, 2 * n_tokens, kv_width),
        ],
        axis=2,
    )
    d_kv_tokens = d_kv.reshape(n_requests, n_tokens, 2 * kv_width).transpose(1, 0, 2)
    summed = jnp.dot(
        d_kv_tokens.reshape(-1, 2 * kv_width), w_kv.T, preferred_element_type=jnp.float32
    )
    share_grad = lax.psum_scatter(
        summed.reshape(tok_share * lax.axis_size("tensor"), n_requests, enc_width),
        "tensor",
        scatter_dimension=0,
        tiled=True,
    )
    back_buffer = jnp.zeros((n_dp * capacity, tok_share, enc_width), jnp.float32)
    back_buffer = back_buffer.at[position].set(share_grad.transpose(1, 0, 2))
    returned = lax.all_to_all(
        back_buffer.reshape(n_dp, capacity, tok_share, enc_width),
        "dp",
        split_axis=0,
        concat_axis=0,
        tiled=True,
    )
    matches = (asked[:, :, None] == jnp.arange(n_slabs, dtype=jnp.int32)[None, None, :]).astype(
        jnp.float32
    )
    d_table = jnp.einsum("pcs,pcte->ste", matches, returned, precision=lax.Precision.HIGHEST)
    return (attended, d_query, d_table)


def solution(mesh):
    in_specs = (
        P("dp", "tensor"),
        P("dp", "tensor"),
        P("dp", None, None),
        P(None, "tensor"),
        P(None, "tensor"),
        P("dp", None),
        P("dp", None),
    )
    out_specs = (P("dp", "tensor"), P("dp", "tensor"), P("dp", "tensor", None))
    return jax.shard_map(
        on_device, mesh=mesh, in_specs=in_specs, out_specs=out_specs, check_vma=False
    )
```

profile of v0, /device:TPU:6, one launch (start us, length us, event | category | flops | bytes accessed | tf_op | source)
XLA Modules:
  0.0 639.2 jit_solution(6673175156596337142)
XLA Ops:
  7.2 0.8 copy.42
  7.9 0.7 broadcast_multiply_fusion
  8.6 0.1 eq.30
  8.7 0.1 fusion.34
  8.8 0.2 select_reduce_fusion
  9.0 0.1 copy.41
  9.1 0.1 mul.32
  9.1 0.8 copy.43
  9.9 0.1 reshape.128
  10.0 0.6 scatter_custom_fusion
  10.6 0.1 all_to_all.12
  10.7 21.0 %all_to_all.19 = s32[32,1,2]{2,1,0:T(1,128)S(1)} all-to-all(s32[32,1,2]{2,1,0:T(1,128)S(1)} %bitcast.107), channel_id=1, replica_groups=mesh['dp'=32,'tensor'=8] {'dp'}, dimensions={0} | all-to-all | bytes 512 | tf_op jit(solution)/shard_map/all_to_all | solution.py:29
  31.7 0.1 maximum_reduce_fusion
  31.8 0.1 reshape.110
  31.9 10.0 %gather_fusion = bf16[64,128,896]{2,1,0:T(8,128)(2,1)} fusion(bf16[16,128,896]{2,1,0:T(8,128)(2,1)} %param.9, s32[1024]{0:T(1024)S(1)} %pad_clamp_fusion.1), kind=kCustom, calls=%fused_computation | custom fusion | bytes 29360384 | tf_op jit(solution)/shard_map/gather | solution.py:34
  41.9 0.0 copy-start.3
  41.9 5.2 all-to-all-start.1
  47.1 0.0 copy-start
  47.1 0.0 copy-start.1
  47.2 0.0 reduce-scatter.2.cloned.1.call-start
  47.2 0.0 copy-done.3
  47.2 0.1 reshape.103
  47.3 1.3 reshape.105
  48.6 0.0 copy-done
  48.6 1.0 constant_dynamic-update-slice_fusion.1
  49.7 0.0 copy-done.1
  49.7 1.0 constant_dynamic-update-slice_fusion
  50.7 319.9 %all-to-all-done.1 = bf16[32,2,128,896]{3,2,1,0:T(8,128)(2,1)} async-done(((bf16[32,2,128,896]{3,2,1,0:T(8,128)(2,1)}), bf16[32,2,128,896]{3,2,1,0:T(8,128)(2,1)}, u32[]{:S(2)}, u32[]{:S(2)}) %all-to-all-start.1) | async-done | bytes 14680096 | tf_op jit(solution)/shard_map/all_to_all | solution.py:35
  370.7 7.9 %gather_fusion.1 = bf16[16,128,896]{2,1,0:T(8,128)(2,1)} fusion(bf16[64,128,896]{2,1,0:T(8,128)(2,1)} %bitcast.4, s32[1024]{0:T(1024)S(1)} %pad_clamp_fusion), kind=kCustom, calls=%fused_computation.1 | custom fusion | bytes 7340096 | tf_op jit(solution)/shard_map/gather | solution.py:36
  378.6 7.1 %convolution_convert_fusion = bf16[2048,1024]{1,0:T(8,128)(2,1)S(1)} fusion(bf16[2048,896]{1,0:T(8,128)(2,1)} %bitcast.103, bf16[896,1024]{1,0:T(8,128)(2,1)} %constant_dynamic-update-slice_fusion), kind=kOutput, calls=%fused_computation.10 | convolution fusion | flops 3760193536 | bytes 9699328 | tf_op jit(solution)/shard_map/dot_general | solution.py:37
  385.7 1.8 fusion.52
  387.5 2.8 copy.75
  390.3 2.0 fusion.29
  392.3 1.9 fusion.53
  394.2 4.0 copy.74
  398.2 3.3 fusion.26
  401.5 5.7 convert_bitcast_fusion
  407.2 17.2 %convert_bitcast_fusion.1 = bf16[8,256,4,128]{3,1,2,0:T(8,128)(2,1)} fusion(f32[8,4,256,64]{2,3,1,0:T(8,128)} %fusion.26, bf16[8,64,4,128]{3,2,1,0:T(4,128)(2,1)S(1)} %reshape.103, f32[8,4,64,256]{3,2,1,0:T(8,128)} %get-tuple-element.15, f32[8,4,64]{2,1,0:T(4,128)S(1)} %get-tuple-element.14), kind=kOutput, calls=%fused_computation.23 | convolution fusion | flops 138938624 | bytes 6823936 | tf_op jit(solution)/shard_map/chqk,cqhd->ckhd/dot_general | solution.py:59
  424.5 4.5 copy.70
  429.0 4.1 reshape.145
  433.1 4.5 copy.71
  437.6 4.3 reshape.146
  441.9 10.3 %fusion.2 = f32[128,16,896]{2,0,1:T(8,128)} fusion(bf16[16,128,512]{2,1,0:T(8,128)(2,1)} %reshape.146, bf16[16,128,512]{2,1,0:T(8,128)(2,1)} %reshape.145, bf16[896,1024]{1,0:T(8,128)(2,1)} %constant_dynamic-update-slice_fusion), kind=kOutput, calls=%fused_computation.7 | convolution fusion | flops 3766484992 | bytes 13369344 | tf_op jit(solution)/shard_map/dot_general | solution.py:73
  452.2 0.0 reduce-scatter.2.cloned.1.call-update
  452.2 68.9 %reduce-scatter.2.cloned.1.call-done = f32[16,16,896]{2,0,1:T(8,128)} async-done(((f32[128,16,896]{2,0,1:T(8,128)}), f32[16,16,896]{2,0,1:T(8,128)}) %reduce-scatter.2.cloned.1.call-update) | async-done | bytes 917520 | tf_op jit(solution)/shard_map/reduce_scatter | solution.py:76
  521.1 0.0 copy-start.2
  521.1 2.1 broadcast_in_dim.5
  523.2 0.0 copy-done.2
  523.2 2.9 scatter_fusion
  526.1 5.7 copy.62
  531.8 10.2 %all-to-all-start.2 = ((f32[32,2,16,896]{3,1,2,0:T(2,128)}), f32[32,2,16,896]{3,1,2,0:T(2,128)}, u32[]{:S(2)}, u32[]{:S(2)}) async-start(f32[32,2,16,896]{3,1,2,0:T(2,128)} %copy.62), calls=%async_computation.3 | async-start | bytes 7340032 | tf_op jit(solution)/shard_map/all_to_all | solution.py:84
  542.0 0.1 copy.55
  542.1 15.5 %fusion.20 = bf16[8,64,4,128]{3,1,2,0:T(8,128)(2,1)S(1)} fusion(bf16[8,256,4,128]{1,3,2,0:T(8,128)(2,1)} %bitcast.101, f32[8,4,256,64]{2,3,1,0:T(8,128)} %fusion.26, f32[8,4,64,256]{3,2,1,0:T(8,128)} %get-tuple-element.15, f32[8,4,64]{2,1,0:T(4,128)S(1)} %get-tuple-element.14), kind=kOutput, calls=%fused_computation.30 | convolution fusion | flops 138152192 | bytes 6823936 | tf_op jit(solution)/shard_map/chqk,ckhd->cqhd/dot_general | solution.py:57
  557.6 0.4 copy.54
  558.0 5.2 fusion.19
  563.3 0.4 copy.50
  563.7 1.1 copy_bitcast_fusion
  564.8 60.8 %all-to-all-done.2 = f32[32,2,16,896]{3,1,2,0:T(2,128)} async-done(((f32[32,2,16,896]{3,1,2,0:T(2,128)}), f32[32,2,16,896]{3,1,2,0:T(2,128)}, u32[]{:S(2)}, u32[]{:S(2)}) %all-to-all-start.2) | async-done | bytes 3670048 | tf_op jit(solution)/shard_map/all_to_all | solution.py:84
  625.6 5.3 fusion.16
  630.9 1.2 copy.64
  (4 shorter events, 0.1 us)
Async XLA Ops:
  41.9 5.3 copy-start.3
  41.9 328.8 %all-to-all-start.1 = ((bf16[32,2,128,896]{3,2,1,0:T(8,128)(2,1)}), bf16[32,2,128,896]{3,2,1,0:T(8,128)(2,1)}, u32[]{:S(2)}, u32[]{:S(2)}) async-start(bf16[32,2,128,896]{3,2,1,0:T(8,128)(2,1)} %bitcast.96), calls=%async_computation.1 | async-start | bytes 29360128 | tf_op jit(solution)/shard_map/all_to_all | solution.py:35
  47.1 1.5 copy-start
  47.1 2.5 copy-start.1
  47.2 474.0 %reduce-scatter.2.cloned.1.call-start = ((), (), s32[]{:S(2)}) async-start(), calls=%async_computation.4 | async-start | bytes 8257536 | tf_op jit(solution)/shard_map/reduce_scatter | solution.py:76
  521.1 2.1 copy-start.2
  531.8 93.8 %all-to-all-start.2 = ((f32[32,2,16,896]{3,1,2,0:T(2,128)}), f32[32,2,16,896]{3,1,2,0:T(2,128)}, u32[]{:S(2)}, u32[]{:S(2)}) async-start(f32[32,2,16,896]{3,1,2,0:T(2,128)} %copy.62), calls=%async_computation.3 | async-start | bytes 7340032 | tf_op jit(solution)/shard_map/all_to_all | solution.py:84
Sparse Core Ops, SparseCore 0:
  452.3 68.7 reduce-scatter.1
where the time goes:
time: 650 us; the launch traced here: 639 us
  waiting for transfers between devices  450 us (69%)
  matrix products  71.7 us (11%)
  local copies, waits for them, and re-layouts  64 us (10%)
  blocking collectives  21 us (3%)
  starting transfers between devices  15.5 us (2%)
  between operations  14.4 us (2%)
    all_to_all x1, waiting for transfers between devices, on_device(): lax.all_to_all(sent_rows, 'dp', split_axis=0, concat_axis=0, tiled=True)  320 us
    reduce_scatter x1, waiting for transfers between devices, on_device(): lax.psum_scatter(summed.reshape(tok_share * lax.axis_size('tensor'), n_re...  68.9 us
    all_to_all x1, waiting for transfers between devices, on_device(): lax.all_to_all(back_buffer.reshape(n_dp, capacity, tok_share, enc_width),...  60.8 us
    all_to_all x1, blocking collectives, on_device(): lax.all_to_all(request_buffer.reshape(n_dp, capacity), 'dp', split_axis=0...  21 us
    concatenate x4, local copies, waits for them, and re-layouts, on_device(): jnp.concatenate([d_keys.reshape(spans, 2 * n_tokens, kv_width), d_values....  17.4 us
    dot_general x1, matrix products, on_device(): jnp.einsum('chqk,cqhd->ckhd', dscores, query_heads, preferred_element_typ...  17.2 us
    dot_general x1, matrix products, on_device(): jnp.einsum('chqk,ckhd->cqhd', dscores, keys, preferred_element_type=jnp.f...  15.5 us
  transfers between devices with their start and end apart: 3, of which 3 were waited for; matrix products, arithmetic and copies ran while one was open for 4% of the time, Pallas kernels for 0%

commit v1 on v0

v1 whole, which is shorter than its diff:
```python
import functools
import math

import jax
import jax.numpy as jnp
from jax import lax
from jax.experimental import pallas as pl
from jax.experimental.pallas import tpu as pltpu
from jax.sharding import PartitionSpec as P

HD = 128
SPAN = 64
LANES = 128
MESH = pl.DeviceIdType.MESH
VMEM_LIMIT = 48 * 1024 * 1024


def cut_lanes(width, small_last):
    cuts = []
    at = 0
    widths = [256] * (width // 256) + ([width % 256] if width % 256 else [])
    if not small_last:
        widths = widths[::-1]
    for w in widths:
        cuts.append((at, w))
        at += w
    return cuts


def greet(me, t, n_dp, n_x):
    x, core = lax.div(t, 2), lax.rem(t, 2)
    barrier = pltpu.get_barrier_semaphore()

    def hello(i, carry):
        pl.semaphore_signal(
            barrier, inc=1, device_id=(lax.rem(me + i, n_dp), t), device_id_type=MESH
        )
        return carry

    lax.fori_loop(1, n_dp, hello, 0)
    for i in range(1, n_x):
        pl.semaphore_signal(
            barrier,
            inc=1,
            device_id=(me, lax.rem(x + i, n_x) * 2 + core),
            device_id_type=MESH,
        )
    pl.semaphore_signal(barrier, inc=1, device_id=(me, x * 2 + 1 - core), device_id_type=MESH)
    pl.semaphore_wait(barrier, n_dp - 1 + n_x - 1 + 1)


def fetch_kernel(n_dp, n_tp, cuts, owners, slots, table, nb, met, *scratch):
    nk = len(cuts)
    share, send, row, met_s = scratch[:4]
    recv = scratch[4 : 4 + nk]
    sel = scratch[4 + nk : 4 + 2 * nk]
    ld_sem, meta_send, meta_recv, a_send, a_recv, x_send, x_recv, m_send, m_recv = scratch[
        4 + 2 * nk :
    ]
    me = lax.axis_index("dp")
    t = lax.axis_index("tensor")
    n_x = n_tp // 2
    x, core = lax.div(t, 2), lax.rem(t, 2)
    mate = x * 2 + 1 - core
    ts = share.shape[1]
    n_req = 2 * owners.shape[0]

    load = pltpu.make_async_copy(table.at[:, pl.ds(t * ts, ts), :], share, ld_sem)
    load.start()

    lane = lax.broadcasted_iota(jnp.int32, (1, LANES), 1)
    lane_dp = lane & (n_dp - 1)
    lane_place = lax.shift_right_logical(lane, int(math.log2(n_dp))) & 1
    is_slot = lane < 2 * n_dp
    asked_row = jnp.full((1, LANES), -1, jnp.int32)
    seen = jnp.zeros((1, LANES), jnp.int32)
    places = []
    own = [owners[r // 2, r % 2] for r in range(n_req)]
    for r in range(n_req):
        hit = lane_dp == own[r]
        asked_row = jnp.where(
            hit & (seen == lane_place), jnp.where(is_slot, slots[r // 2, r % 2], r), asked_row
        )
        seen = seen + hit.astype(jnp.int32)
        before = jnp.int32(0)
        for other in range(r):
            before = before + jnp.where(own[other] == own[r], 1, 0)
        places.append(2 * own[r] + before)
    row[...] = asked_row

    greet(me, t, n_dp, n_x)

    def meta_copy(peer, slot, sem_slot):
        return pltpu.make_async_remote_copy(
            src_ref=row,
            dst_ref=met.at[slot],
            send_sem=meta_send.at[peer],
            recv_sem=meta_recv.at[sem_slot],
            device_id=(peer, t),
            device_id_type=MESH,
        )

    def start_meta(i, carry):
        meta_copy(lax.rem(me + i, n_dp), me, me).start()
        return carry

    lax.fori_loop(1, n_dp, start_meta, 0)
    met[me] = asked_row

    def wait_meta(i, carry):
        peer = lax.rem(me + i, n_dp)
        meta_copy(peer, peer, peer).wait_recv()
        meta_copy(peer, me, me).wait_send()
        return carry

    lax.fori_loop(1, n_dp, wait_meta, 0)
    to_smem = pltpu.make_async_copy(met, met_s, ld_sem)
    load.wait()
    to_smem.start()
    to_smem.wait()

    def pair_copy(k, peer, slot):
        lo, w = cuts[k]
        return pltpu.make_async_remote_copy(
            src_ref=send.at[pl.ds(2 * peer, 2), :, pl.ds(lo, w)],
            dst_ref=recv[k].at[pl.ds(2 * slot, 2)],
            send_sem=a_send.at[k, peer],
            recv_sem=a_recv.at[k, slot],
            device_id=(peer, t),
            device_id_type=MESH,
        )

    for k, (lo, w) in enumerate(cuts):
        def start_pair(i, carry, k=k, lo=lo, w=w):
            peer = lax.rem(me + i, n_dp)
            for c in range(2):
                index = jnp.maximum(met_s[peer, 0, c * n_dp + me], 0)
                send[2 * peer + c, :, lo : lo + w] = share[index, :, lo : lo + w]
            pair_copy(k, peer, me).start()
            return carry

        lax.fori_loop(1, n_dp, start_pair, 0)
        for c in range(2):
            index = jnp.maximum(met_s[me, 0, c * n_dp + me], 0)
            recv[k][2 * me + c] = share[index, :, lo : lo + w]

    def tensor_copy(k, src, owner_t, peer_t, send_sem, recv_sem):
        lo, w = cuts[k]
        return pltpu.make_async_remote_copy(
            src_ref=src,
            dst_ref=nb.at[:, pl.ds(owner_t * ts, ts), pl.ds(lo, w)],
            send_sem=send_sem,
            recv_sem=recv_sem,
            device_id=(me, peer_t),
            device_id_type=MESH,
        )

    def forward(k):
        lo, w = cuts[k]
        for i in range(1, n_x):
            far = lax.rem(x + n_x - i, n_x) * 2 + core
            tensor_copy(k, sel[k], far, far, x_send.at[k, i], x_recv.at[k, i]).wait_recv()
            tensor_copy(
                k,
                nb.at[:, pl.ds(far * ts, ts), pl.ds(lo, w)],
                far,
                mate,
                m_send.at[k, i],
                m_recv.at[k, i],
            ).start()

    for k, (lo, w) in enumerate(cuts):
        def wait_pair(i, carry, k=k):
            peer = lax.rem(me + i, n_dp)
            pair_copy(k, peer, peer).wait_recv()
            return carry

        lax.fori_loop(1, n_dp, wait_pair, 0)
        for r in range(n_req):
            sel[k][r] = recv[k][places[r]]
        for i in range(1, n_x):
            near = lax.rem(x + i, n_x) * 2 + core
            tensor_copy(k, sel[k], t, near, x_send.at[k, i], x_recv.at[k, i]).start()
        tensor_copy(k, sel[k], t, mate, m_send.at[k, 0], m_recv.at[k, 0]).start()
        nb[:, pl.ds(pl.multiple_of(t * ts, ts), ts), lo : lo + w] = sel[k][...]
        if k > 0:
            forward(k - 1)
    forward(nk - 1)

    for k, (lo, w) in enumerate(cuts):
        for i in range(n_x):
            far = lax.rem(x + n_x - i, n_x) * 2
            tensor_copy(
                k, sel[k], far + 1 - core, mate, m_send.at[k, i], m_recv.at[k, i]
            ).wait_recv()
            tensor_copy(k, sel[k], far + core, mate, m_send.at[k, i], m_recv.at[k, i]).wait_send()
            if i > 0:
                tensor_copy(
                    k, sel[k], t, mate, x_send.at[k, i], x_recv.at[k, i]
                ).wait_send()

        def drain(i, carry, k=k):
            pair_copy(k, lax.rem(me + i, n_dp), me).wait_send()
            return carry

        lax.fori_loop(1, n_dp, drain, 0)


def fetch(n_dp, n_tp, owners, slots, table):
    n_slabs, n_tokens, enc = table.shape
    ts = n_tokens // n_tp
    n_req = 2 * owners.shape[0]
    n_x = n_tp // 2
    cuts = cut_lanes(enc, True)
    nk = len(cuts)
    dma = pltpu.SemaphoreType.DMA
    return pl.pallas_call(
        functools.partial(fetch_kernel, n_dp, n_tp, cuts),
        out_shape=[
            jax.ShapeDtypeStruct((n_req, n_tokens, enc), table.dtype),
            jax.ShapeDtypeStruct((n_dp, 1, LANES), jnp.int32),
        ],
        in_specs=[
            pl.BlockSpec(memory_space=pltpu.SMEM),
            pl.BlockSpec(memory_space=pltpu.SMEM),
            pl.BlockSpec(memory_space=pl.ANY),
        ],
        out_specs=[
            pl.BlockSpec(memory_space=pltpu.VMEM),
            pl.BlockSpec(memory_space=pltpu.VMEM),
        ],
        scratch_shapes=[
            pltpu.VMEM((n_slabs, ts, enc), table.dtype),
            pltpu.VMEM((2 * n_dp, ts, enc), table.dtype),
            pltpu.VMEM((1, LANES), jnp.int32),
            pltpu.SMEM((n_dp, 1, LANES), jnp.int32),
        ]
        + [pltpu.VMEM((2 * n_dp, ts, w), table.dtype) for _, w in cuts]
        + [pltpu.VMEM((n_req, ts, w), table.dtype) for _, w in cuts]
        + [
            dma,
            dma((n_dp,)),
            dma((n_dp,)),
            dma((nk, n_dp)),
            dma((nk, n_dp)),
            dma((nk, n_x)),
            dma((nk, n_x)),
            dma((nk, n_x)),
            dma((nk, n_x)),
        ],
        compiler_params=pltpu.CompilerParams(
            collective_id=0, has_side_effects=True, vmem_limit_bytes=VMEM_LIMIT
        ),
        name="fetch",
    )(owners, slots, table)


def nt(a, b):
    return lax.dot_general(a, b, (((1,), (1,)), ((), ())), preferred_element_type=jnp.float32)


def tn(a, b):
    return lax.dot_general(a, b, (((0,), (0,)), ((), ())), preferred_element_type=jnp.float32)


def nn(a, b):
    return lax.dot_general(a, b, (((1,), (0,)), ((), ())), preferred_element_type=jnp.float32)


def attend_kernel(n_tp, q_ref, g_ref, nb_ref, wk_ref, wv_ref, att_ref, dq_ref, dn_ref):
    bf16 = jnp.bfloat16
    n_tokens, enc = nb_ref.shape[1:]
    ts = n_tokens // n_tp
    scale = 1.0 / math.sqrt(HD)
    width = q_ref.shape[1]
    heads = width // HD
    rows = nb_ref[...].reshape(2 * n_tokens, enc)
    keys = nn(rows, wk_ref[...]).astype(bf16)
    values = nn(rows, wv_ref[...]).astype(bf16)
    q = q_ref[...]
    g = g_ref[...]
    cut = [slice(h * HD, (h + 1) * HD) for h in range(heads)]
    scores = jnp.concatenate([nt(q[:, s], keys[:, s]) for s in cut], axis=0) * scale
    d_weights = jnp.concatenate([nt(g[:, s], values[:, s]) for s in cut], axis=0)
    e = jnp.exp(scores - jnp.max(scores, axis=1, keepdims=True))
    probs = e / jnp.sum(e, axis=1, keepdims=True)
    row_sums = jnp.sum(d_weights * probs, axis=1, keepdims=True)
    ds = (probs * (d_weights - row_sums) * scale).astype(bf16)
    weights = probs.astype(bf16)
    d_keys = []
    d_values = []
    for h, s in enumerate(cut):
        w_h = weights[h * SPAN : (h + 1) * SPAN]
        ds_h = ds[h * SPAN : (h + 1) * SPAN]
        att_ref[:, s] = nn(w_h, values[:, s]).astype(bf16)
        dq_ref[:, s] = nn(ds_h, keys[:, s]).astype(bf16)
        d_keys.append(tn(ds_h, q[:, s]).astype(bf16))
        d_values.append(tn(w_h, g[:, s]).astype(bf16))
    dn = nt(jnp.concatenate(d_keys, axis=1), wk_ref[...])
    dn = dn + nt(jnp.concatenate(d_values, axis=1), wv_ref[...])
    dn = dn.astype(bf16)
    for rr in range(2):
        for t in range(n_tp):
            at = rr * n_tokens + t * ts
            dn_ref[t % 2, t // 2, rr] = dn[at : at + ts]


def attend(n_tp, queries, cotangent, nb, key_weight, value_weight):
    n_req, n_tokens, enc = nb.shape
    spans = n_req // 2
    width = queries.shape[1]
    ts = n_tokens // n_tp
    whole = lambda c: (0, 0)
    return pl.pallas_call(
        functools.partial(attend_kernel, n_tp),
        grid=(spans,),
        out_shape=[
            jax.ShapeDtypeStruct(queries.shape, jnp.bfloat16),
            jax.ShapeDtypeStruct(queries.shape, jnp.bfloat16),
            jax.ShapeDtypeStruct((2, n_tp // 2, n_req, ts, enc), jnp.bfloat16),
        ],
        in_specs=[
            pl.BlockSpec((SPAN, width), lambda c: (c, 0)),
            pl.BlockSpec((SPAN, width), lambda c: (c, 0)),
            pl.BlockSpec((2, n_tokens, enc), lambda c: (c, 0, 0)),
            pl.BlockSpec(key_weight.shape, whole),
            pl.BlockSpec(value_weight.shape, whole),
        ],
        out_specs=[
            pl.BlockSpec((SPAN, width), lambda c: (c, 0)),
            pl.BlockSpec((SPAN, width), lambda c: (c, 0)),
            pl.BlockSpec((2, n_tp // 2, 2, ts, enc), lambda c: (0, 0, c, 0, 0)),
        ],
        compiler_params=pltpu.CompilerParams(vmem_limit_bytes=VMEM_LIMIT),
        name="attend",
    )(queries, cotangent, nb, key_weight, value_weight)


def give_back_kernel(n_dp, n_tp, cuts, met, dn, got, *scratch):
    nk = len(cuts)
    mrecv = scratch[:nk]
    chip = scratch[nk : 2 * nk]
    xrecv = scratch[2 * nk : 3 * nk]
    total = scratch[3 * nk : 4 * nk]
    send = scratch[4 * nk : 5 * nk]
    a_send, a_recv, x_send, x_recv, m_send, m_recv = scratch[5 * nk :]
    me = lax.axis_index("dp")
    t = lax.axis_index("tensor")
    n_x = n_tp // 2
    x, core = lax.div(t, 2), lax.rem(t, 2)
    mate = x * 2 + 1 - core
    n_req = dn.shape[2]

    greet(me, t, n_dp, n_x)

    def mate_copy(k):
        lo, w = cuts[k]
        return pltpu.make_async_remote_copy(
            src_ref=dn.at[1 - core, :, :, :, pl.ds(lo, w)],
            dst_ref=mrecv[k],
            send_sem=m_send.at[k],
            recv_sem=m_recv.at[k],
            device_id=(me, mate),
            device_id_type=MESH,
        )

    def x_copy(k, i):
        far = lax.rem(x + i, n_x)
        return pltpu.make_async_remote_copy(
            src_ref=chip[k].at[far],
            dst_ref=xrecv[k].at[i - 1],
            send_sem=x_send.at[k, i],
            recv_sem=x_recv.at[k, i],
            device_id=(me, far * 2 + core),
            device_id_type=MESH,
        )

    def pair_copy(k, peer, slot):
        lo, w = cuts[k]
        return pltpu.make_async_remote_copy(
            src_ref=send[k].at[pl.ds(2 * peer, 2)],
            dst_ref=got.at[pl.ds(2 * slot, 2), :, pl.ds(lo, w)],
            send_sem=a_send.at[k, peer],
            recv_sem=a_recv.at[k, slot],
            device_id=(peer, t),
            device_id_type=MESH,
        )

    for k in range(nk):
        mate_copy(k).start()

    def pair_sum(k):
        lo, w = cuts[k]
        mate_copy(k).wait_recv()

        def add_rows(j, carry):
            for to in range(n_x):
                both = dn[core, to, j, :, lo : lo + w].astype(jnp.float32) + mrecv[k][
                    to, j
                ].astype(jnp.float32)
                chip[k][to, j] = both.astype(jnp.bfloat16)
            return carry

        lax.fori_loop(0, n_req, add_rows, 0)
        for i in range(1, n_x):
            x_copy(k, i).start()

    def scatter(k):
        lo, w = cuts[k]
        for i in range(1, n_x):
            x_copy(k, i).wait_recv()

        def add_rows(j, carry):
            sum_f = chip[k][x, j].astype(jnp.float32)
            for i in range(1, n_x):
                sum_f = sum_f + xrecv[k][i - 1, j].astype(jnp.float32)
            total[k][j] = sum_f.astype(jnp.bfloat16)
            return carry

        lax.fori_loop(0, n_req, add_rows, 0)

        def start_pair(i, carry):
            peer = lax.rem(me + i, n_dp)
            for c in range(2):
                index = jnp.maximum(met[me, 0, (2 + c) * n_dp + peer], 0)
                send[k][2 * peer + c] = total[k][index]
            pair_copy(k, peer, me).start()
            return carry

        lax.fori_loop(1, n_dp, start_pair, 0)
        for c in range(2):
            index = jnp.maximum(met[me, 0, (2 + c) * n_dp + me], 0)
            got[2 * me + c, :, lo : lo + w] = total[k][index]

    pair_sum(0)
    for k in range(nk):
        if k + 1 < nk:
            pair_sum(k + 1)
        scatter(k)

    for k in range(nk):
        mate_copy(k).wait_send()
        for i in range(1, n_x):
            x_copy(k, i).wait_send()

        def drain(i, carry, k=k):
            peer = lax.rem(me + i, n_dp)
            pair_copy(k, peer, me).wait_send()
            pair_copy(k, peer, peer).wait_recv()
            return carry

        lax.fori_loop(1, n_dp, drain, 0)


def give_back(n_dp, n_tp, met, dn):
    _, n_x, n_req, ts, enc = dn.shape
    cuts = cut_lanes(enc, False)
    nk = len(cuts)
    dma = pltpu.SemaphoreType.DMA
    bf16 = jnp.bfloat16
    return pl.pallas_call(
        functools.partial(give_back_kernel, n_dp, n_tp, cuts),
        out_shape=jax.ShapeDtypeStruct((2 * n_dp, ts, enc), bf16),
        in_specs=[
            pl.BlockSpec(memory_space=pltpu.SMEM),
            pl.BlockSpec(memory_space=pltpu.VMEM),
        ],
        out_specs=pl.BlockSpec(memory_space=pltpu.VMEM),
        scratch_shapes=[pltpu.VMEM((n_x, n_req, ts, w), bf16) for _, w in cuts]
        + [pltpu.VMEM((n_x, n_req, ts, w), bf16) for _, w in cuts]
        + [pltpu.VMEM((n_x - 1, n_req, ts, w), bf16) for _, w in cuts]
        + [pltpu.VMEM((n_req, ts, w), bf16) for _, w in cuts]
        + [pltpu.VMEM((2 * n_dp, ts, w), bf16) for _, w in cuts]
        + [
            dma((nk, n_dp)),
            dma((nk, n_dp)),
            dma((nk, n_x)),
            dma((nk, n_x)),
            dma((nk,)),
            dma((nk,)),
        ],
        compiler_params=pltpu.CompilerParams(
            collective_id=1, has_side_effects=True, vmem_limit_bytes=VMEM_LIMIT
        ),
        name="give_back",
    )(met, dn)


def collect_kernel(n_dp, met, got, out):
    me = lax.axis_index("dp")
    out[...] = jnp.zeros(out.shape, jnp.float32)

    def add(p, carry):
        for c in range(2):
            slab = met[p, 0, c * n_dp + me]

            @pl.when(slab >= 0)
            def _():
                out[slab] = out[slab] + got[2 * p + c].astype(jnp.float32)

        return carry

    lax.fori_loop(0, n_dp, add, 0)


def collect(n_dp, n_slabs, met, got):
    _, ts, enc = got.shape
    return pl.pallas_call(
        functools.partial(collect_kernel, n_dp),
        out_shape=jax.ShapeDtypeStruct((n_slabs, ts, enc), jnp.float32),
        in_specs=[
            pl.BlockSpec(memory_space=pltpu.SMEM),
            pl.BlockSpec(memory_space=pltpu.VMEM),
        ],
        out_specs=pl.BlockSpec(memory_space=pltpu.VMEM),
        name="collect",
    )(met, got)


def on_device(queries, cotangent, table, key_weight, value_weight, owners, slots):
    n_dp = lax.axis_size("dp")
    n_tp = lax.axis_size("tensor")
    nb, met = fetch(n_dp, n_tp, owners, slots, table)
    attended, d_query, dn = attend(n_tp, queries, cotangent, nb, key_weight, value_weight)
    got = give_back(n_dp, n_tp, met, dn)
    d_table = collect(n_dp, table.shape[0], met, got)
    return (attended, d_query, d_table)


def solution(mesh):
    in_specs = (
        P("dp", "tensor"),
        P("dp", "tensor"),
        P("dp", None, None),
        P(None, "tensor"),
        P(None, "tensor"),
        P("dp", None),
        P("dp", None),
    )
    out_specs = (P("dp", "tensor"), P("dp", "tensor"), P("dp", "tensor", None))
    return jax.shard_map(
        on_device, mesh=mesh, in_specs=in_specs, out_specs=out_specs, check_vma=False
    )
```

time: 650 us -> 159 us (0.24); the launches traced: 639 us -> 157 us
  waiting for transfers between devices: 450 us -> 0 us
  Pallas kernels: 0 us -> 149 us
  matrix products: 71.7 us -> 0 us
  local copies, waits for them, and re-layouts: 64 us -> 6.74 us
  blocking collectives: 21 us -> 0 us
  starting transfers between devices: 15.5 us -> 0 us
  between operations: 14.4 us -> 0.72 us
    all_to_all x2 -> x0, waiting for transfers between devices: 381 us -> none  [the longest x1 320 us: on_device(): lax.all_to_all(sent_rows, 'dp', split_axis=0, concat_axis=0, tiled=True)]
    pallas_call x0 -> x4, Pallas kernels: none -> 149 us  [the longest x1 69 us: fetch(): pl.pallas_call(functools.partial(fetch_kernel, n_dp, n_tp, cuts), out_sha...]
    dot_general x9 -> x0, matrix products: 71.7 us -> none  [the longest x1 17.2 us: on_device(): jnp.einsum('chqk,cqhd->ckhd', dscores, query_heads, preferred_element_typ...]
    reduce_scatter x1 -> x0, waiting for transfers between devices: 68.9 us -> none  [on_device(): lax.psum_scatter(summed.reshape(tok_share * lax.axis_size('tensor'), n_re...]
    all_to_all x1 -> x0, blocking collectives: 21 us -> none  [on_device(): lax.all_to_all(request_buffer.reshape(n_dp, capacity), 'dp', split_axis=0...]
    concatenate x5 -> x0, local copies, waits for them, and re-layouts: 18.5 us -> none  [the longest x4 17.4 us: on_device(): jnp.concatenate([d_keys.reshape(spans, 2 * n_tokens, kv_width), d_values....]
    gather x2 -> x0, local copies, waits for them, and re-layouts: 17.9 us -> none  [the longest x1 9.97 us: on_device(): sent_rows = table[safe_slot]]
    all_to_all x2 -> x0, starting transfers between devices: 15.4 us -> none  [the longest x1 10.2 us: on_device(): lax.all_to_all(back_buffer.reshape(n_dp, capacity, tok_share, enc_width),...]
  transfers between devices with their start and end apart: 3 -> 0, of which waited for: 3 -> 0; matrix products, arithmetic and copies ran while one was open for 4% -> 0% of each run, Pallas kernels for 0% -> 0%
where the time goes in v1:
time: 159 us; the launch traced here: 157 us
  Pallas kernels  149 us (94%)
  local copies, waits for them, and re-layouts  6.74 us (4%)
    pallas_call x1, Pallas kernels, fetch(): pl.pallas_call(functools.partial(fetch_kernel, n_dp, n_tp, cuts), out_sha...  69 us
    pallas_call x1, Pallas kernels, give_back(): pl.pallas_call(functools.partial(give_back_kernel, n_dp, n_tp, cuts), out...  58.2 us
    pallas_call x1, Pallas kernels, attend(): pl.pallas_call(functools.partial(attend_kernel, n_tp), grid=(spans,), out...  18.6 us
    unnamed x18, local copies, waits for them, and re-layouts  6.74 us
    pallas_call x1, Pallas kernels, collect(): pl.pallas_call(functools.partial(collect_kernel, n_dp), out_shape=jax.Sha...  3.42 us

profile of v1, /device:TPU:6, one launch (start us, length us, event | category | flops | bytes accessed | tf_op | source)
XLA Modules:
  0.0 156.7 jit_solution(16522885937481552898)
XLA Ops:
  0.6 0.0 copy-start.4
  0.6 0.0 copy-start.3
  0.7 0.0 copy-start.6
  0.7 0.0 copy-start.5
  0.7 0.9 copy.10.owners
  1.6 0.8 copy.11.slots
  2.3 69.0 %fetch.1 = (bf16[16,128,896]{2,1,0:T(8,128)(2,1)S(1)}, s32[32,1,128]{2,1,0:T(1,128)S(1)}) custom-call(s32[8,2]{1,0:T(8,128)S(1)} %copy.10.owners, s32[8,2]{1,0:T(8,128)S(1)} %copy.11.slots, bf16[16,128,896]{2,1,0:T(8,128)(2,1)} %table.1), custom_call_target="tpu_custom_call" | custom-call | tf_op jit(solution)/shard_map/fetch/pallas_call | solution.py:217
  71.3 0.0 copy-start.1
  71.3 1.8 %copy-done.1 = bf16[16,128,896]{2,1,0:T(8,128)(2,1)} copy-done((bf16[16,128,896]{2,1,0:T(8,128)(2,1)}, bf16[16,128,896]{2,1,0:T(8,128)(2,1)S(1)}, u32[]{:S(2)}) %copy-start.1) | copy-done | bytes 3670040
  73.1 0.0 copy-start.7
  73.1 0.0 copy-done.4
  73.1 0.0 copy-done.3
  73.1 0.0 copy-done.6
  73.1 0.0 copy-done.5
  73.1 18.6 %attend.1 = (bf16[512,512]{1,0:T(8,128)(2,1)}, bf16[512,512]{1,0:T(8,128)(2,1)}, bf16[2,4,16,16,896]{4,3,2,1,0:T(8,128)(2,1)}) custom-call(bf16[512,512]{1,0:T(8,128)(2,1)S(1)} %copy-done.5, bf16[512,512]{1,0:T(8,128)(2,1)S(1)} %copy-done.6, bf16[16,128,896]{2,1,0:T(8,128)(2,1)} %copy-done.1, bf16[896,512]{1,0:T(8,128)(2,1)S(1)} %copy-done.3, ...), custom_call_target="tpu_custom_call" | custom-call | tf_op jit(solution)/shard_map/attend/pallas_call | solution.py:314
  91.7 0.0 copy-start.2
  91.7 2.0 %copy-done.2 = bf16[2,4,16,16,896]{4,3,2,1,0:T(8,128)(2,1)S(1)} copy-done((bf16[2,4,16,16,896]{4,3,2,1,0:T(8,128)(2,1)S(1)}, bf16[2,4,16,16,896]{4,3,2,1,0:T(8,128)(2,1)}, u32[]{:S(2)}) %copy-start.2) | copy-done | bytes 3670040
  93.8 58.2 %give_back.1.got = bf16[64,16,896]{2,1,0:T(8,128)(2,1)S(1)} custom-call(s32[32,1,128]{2,1,0:T(1,128)S(1)} %get-tuple-element.11.met, bf16[2,4,16,16,896]{4,3,2,1,0:T(8,128)(2,1)S(1)} %copy-done.2), custom_call_target="tpu_custom_call" | custom-call | tf_op jit(solution)/shard_map/give_back/pallas_call | solution.py:461
  152.0 0.0 copy-done.7
  152.0 0.0 copy-start
  152.0 1.2 copy-done
  153.3 3.4 %collect.1 = f32[16,16,896]{2,1,0:T(8,128)} custom-call(s32[32,1,128]{2,1,0:T(1,128)} %copy-done.7, bf16[64,16,896]{2,1,0:T(8,128)(2,1)} %copy-done), custom_call_target="tpu_custom_call" | custom-call | tf_op jit(solution)/shard_map/collect/pallas_call | solution.py:508
Async XLA Ops:
  0.6 72.5 %copy-start.4 = (bf16[896,512]{1,0:T(8,128)(2,1)S(1)}, bf16[896,512]{1,0:T(8,128)(2,1)}, u32[]{:S(2)}) copy-start(bf16[896,512]{1,0:T(8,128)(2,1)} %wv_ref.1) | copy-start | bytes 2752516
  0.6 72.5 %copy-start.3 = (bf16[896,512]{1,0:T(8,128)(2,1)S(1)}, bf16[896,512]{1,0:T(8,128)(2,1)}, u32[]{:S(2)}) copy-start(bf16[896,512]{1,0:T(8,128)(2,1)} %wk_ref.1) | copy-start | bytes 2752516
  0.7 72.5 %copy-start.6 = (bf16[512,512]{1,0:T(8,128)(2,1)S(1)}, bf16[512,512]{1,0:T(8,128)(2,1)}, u32[]{:S(2)}) copy-start(bf16[512,512]{1,0:T(8,128)(2,1)} %g_ref.1) | copy-start | bytes 1572868
  0.7 72.5 %copy-start.5 = (bf16[512,512]{1,0:T(8,128)(2,1)S(1)}, bf16[512,512]{1,0:T(8,128)(2,1)}, u32[]{:S(2)}) copy-start(bf16[512,512]{1,0:T(8,128)(2,1)} %q_ref.1) | copy-start | bytes 1572868
  71.3 1.8 %copy-start.1 = (bf16[16,128,896]{2,1,0:T(8,128)(2,1)}, bf16[16,128,896]{2,1,0:T(8,128)(2,1)S(1)}, u32[]{:S(2)}) copy-start(bf16[16,128,896]{2,1,0:T(8,128)(2,1)S(1)} %get-tuple-element.8.nb_ref) | copy-start | bytes 11010052
  73.1 78.9 %copy-start.7 = (s32[32,1,128]{2,1,0:T(1,128)}, s32[32,1,128]{2,1,0:T(1,128)S(1)}, u32[]{:S(2)}) copy-start(s32[32,1,128]{2,1,0:T(1,128)S(1)} %get-tuple-element.11.met) | copy-start | bytes 49156
  91.7 2.0 %copy-start.2 = (bf16[2,4,16,16,896]{4,3,2,1,0:T(8,128)(2,1)S(1)}, bf16[2,4,16,16,896]{4,3,2,1,0:T(8,128)(2,1)}, u32[]{:S(2)}) copy-start(bf16[2,4,16,16,896]{4,3,2,1,0:T(8,128)(2,1)} %get-tuple-element.12.dn) | copy-start | bytes 11010052
  152.0 1.2 copy-start

commit v2 on v0

v2 whole, which is shorter than its diff:
```python
import functools
import math

import jax
import jax.numpy as jnp
from jax import lax
from jax.experimental import pallas as pl
from jax.experimental.pallas import tpu as pltpu
from jax.sharding import PartitionSpec as P

HD = 128
SPAN = 64
LANES = 128
N_Y = 4
N_Z = 8
HOPS = 6
LAG = 3
AHEAD = 4
FWD_GROUPS = ((6, 2), (5, 3), (4,), (1, 7, 0))
BWD_GROUPS = ((0, 1, 7), (4,), (3, 5), (2, 6))
BWD_READY = {1: 0, 4: 1, 5: 2, 6: 3}
MESH = pl.DeviceIdType.MESH
VMEM_LIMIT = 56 * 1024 * 1024


def lane_chunks(enc):
    units = enc // LANES
    first = (units + 1) // 2
    chunks = []
    at = 0
    for half, count in ((0, first), (1, units - first)):
        for n in ((count + 1) // 2, count // 2):
            if n:
                chunks.append((at * LANES, n * LANES, half))
                at += n
    return chunks


def ring_order(chunks, last):
    ops = [(s, k) for s in range(1, last + 1) for k in range(len(chunks))]
    return sorted(ops, key=lambda o: (o[0] + LAG * chunks[o[1]][2], chunks[o[1]][2], o[1]))


def find_group(groups, d):
    for g, members in enumerate(groups):
        if d in members:
            return g, members.index(d)


def nt(a, b):
    return lax.dot_general(a, b, (((1,), (1,)), ((), ())), preferred_element_type=jnp.float32)


def tn(a, b):
    return lax.dot_general(a, b, (((0,), (0,)), ((), ())), preferred_element_type=jnp.float32)


def nn(a, b):
    return lax.dot_general(a, b, (((1,), (0,)), ((), ())), preferred_element_type=jnp.float32)


def span_grads(q, g, rows, wk, wv):
    bf16 = jnp.bfloat16
    scale = 1.0 / math.sqrt(HD)
    heads = q.shape[1] // HD
    keys = nn(rows, wk).astype(bf16)
    values = nn(rows, wv).astype(bf16)
    cut = [slice(h * HD, (h + 1) * HD) for h in range(heads)]
    scores = jnp.concatenate([nt(q[:, s], keys[:, s]) for s in cut], axis=0) * scale
    d_weights = jnp.concatenate([nt(g[:, s], values[:, s]) for s in cut], axis=0)
    e = jnp.exp(scores - jnp.max(scores, axis=1, keepdims=True))
    probs = e / jnp.sum(e, axis=1, keepdims=True)
    row_sums = jnp.sum(d_weights * probs, axis=1, keepdims=True)
    ds = (probs * (d_weights - row_sums) * scale).astype(bf16)
    weights = probs.astype(bf16)
    attended, d_query, d_keys, d_values = [], [], [], []
    for h, s in enumerate(cut):
        w_h = weights[h * SPAN : (h + 1) * SPAN]
        ds_h = ds[h * SPAN : (h + 1) * SPAN]
        attended.append(nn(w_h, values[:, s]).astype(bf16))
        d_query.append(nn(ds_h, keys[:, s]).astype(bf16))
        d_keys.append(tn(ds_h, q[:, s]).astype(bf16))
        d_values.append(tn(w_h, g[:, s]).astype(bf16))
    dn = nt(jnp.concatenate(d_keys, axis=1), wk) + nt(jnp.concatenate(d_values, axis=1), wv)
    return (
        jnp.concatenate(attended, axis=1),
        jnp.concatenate(d_query, axis=1),
        dn.astype(bf16),
    )


def fused_kernel(
    n_dp, n_tp, treedef, owners, slots, table, queries, cotangent, key_weight, value_weight, att, dq, dt, *flat
):
    b = jax.tree_util.tree_unflatten(treedef, flat)
    bf16 = jnp.bfloat16
    me = lax.axis_index("dp")
    t = lax.axis_index("tensor")
    z, y = lax.div(me, N_Y), lax.rem(me, N_Y)
    n_x = n_tp // 2
    x, core = lax.div(t, 2), lax.rem(t, 2)
    mate = x * 2 + 1 - core
    n_req, ts, enc = b["sel"].shape
    spans = n_req // 2
    side = n_req // 2
    n_tokens = ts * n_tp
    chunks = lane_chunks(enc)
    nk = len(chunks)
    first_w = sum(w for _, w, half in chunks if half == 0)
    halves = ((0, first_w), (first_w, enc - first_w))

    def up(d):
        return lax.rem(z + d, N_Z)

    def send_to(src, dst, ss, rs, dp_to, t_to):
        return pltpu.make_async_remote_copy(
            src_ref=src, dst_ref=dst, send_sem=ss, recv_sem=rs, device_id=(dp_to, t_to), device_id_type=MESH
        )

    loads = [
        pltpu.make_async_copy(table.at[:, pl.ds(t * ts, ts), :], b["share"], b["load_sem"].at[0]),
        pltpu.make_async_copy(key_weight, b["wk"], b["load_sem"].at[1]),
        pltpu.make_async_copy(value_weight, b["wv"], b["load_sem"].at[2]),
        pltpu.make_async_copy(queries, b["q"], b["load_sem"].at[3]),
        pltpu.make_async_copy(cotangent, b["g"], b["load_sem"].at[4]),
    ]
    for load in loads:
        load.start()

    barrier = pltpu.get_barrier_semaphore()
    peers = (
        [(up(d) * N_Y + y, t) for d in range(1, N_Z)]
        + [(z * N_Y + lax.rem(y + i, N_Y), t) for i in range(1, N_Y)]
        + [(me, lax.rem(x + i, n_x) * 2 + core) for i in range(1, n_x)]
        + [(me, mate)]
    )
    for peer in peers:
        pl.semaphore_signal(barrier, inc=1, device_id=peer, device_id_type=MESH)

    lane = lax.broadcasted_iota(jnp.int32, (1, LANES), 1)
    lane_dp = lane & (n_dp - 1)
    lane_place = lax.shift_right_logical(lane, int(math.log2(n_dp))) & 1
    is_slot = lane < 2 * n_dp
    own = [owners[r % 2, r // 2] for r in range(n_req)]
    far = [lax.rem(z - lax.div(own[r], N_Y) + N_Z, N_Z) for r in range(n_req)]
    key = [jnp.where(far[r] == 0, N_Z // 2, far[r]) for r in range(n_req)]
    asked_row = jnp.full((1, LANES), -1, jnp.int32)
    list_row = jnp.zeros((1, LANES), jnp.int32)
    seen = jnp.zeros((1, LANES), jnp.int32)
    ranks = []
    for r in range(n_req):
        before = jnp.int32(0)
        rank = jnp.int32(0)
        for other in range(n_req):
            if other < r:
                before = before + jnp.where(own[other] == own[r], 1, 0)
                rank = rank + jnp.where(key[other] <= key[r], 1, 0)
            elif other > r:
                rank = rank + jnp.where(key[other] < key[r], 1, 0)
        ranks.append(rank)
        hit = lane_dp == own[r]
        asked_row = jnp.where(
            hit & (seen == lane_place), jnp.where(is_slot, slots[r % 2, r // 2], rank), asked_row
        )
        seen = seen + hit.astype(jnp.int32)
        list_row = jnp.where(lane == rank, 2 * own[r] + before, list_row)
        list_row = jnp.where(lane == rank + n_req, r, list_row)
    my_rows = jnp.concatenate([asked_row, list_row], axis=0)
    b["row"][...] = my_rows

    pl.semaphore_wait(barrier, len(peers))

    met, met_s = b["met"], b["met_s"]
    for d in range(1, N_Z):
        send_to(
            b["row"], met.at[y, z], b["meta_send"].at[d], b["meta_recv"].at[d], up(d) * N_Y + y, t
        ).start()
    met[y, z] = my_rows
    for d in range(1, N_Z):
        send_to(
            b["row"], met.at[y, up(N_Z - d)], b["meta_send"].at[d], b["meta_recv"].at[d], up(d) * N_Y + y, t
        ).wait()

    def meta_y(i, from_y):
        return send_to(
            met.at[from_y],
            met.at[from_y],
            b["meta_send"].at[N_Z + i],
            b["meta_recv"].at[N_Z + i],
            z * N_Y + lax.rem(y + i, N_Y),
            t,
        )

    for i in range(1, N_Y):
        meta_y(i, y).start()
    for i in range(1, N_Y):
        meta_y(i, lax.rem(y + N_Y - i, N_Y)).wait_recv()
        meta_y(i, y).wait_send()
    to_smem = pltpu.make_async_copy(met, met_s, b["load_sem"].at[5])
    loads[0].wait()
    to_smem.start()
    to_smem.wait()

    share = b["share"]

    def y_copy(k, g, i, from_y):
        return send_to(
            b["y_out"][k][g].at[i - 1],
            b["cand"][k][g].at[from_y],
            b["y_send"].at[k, g, i],
            b["y_recv"].at[k, g, i],
            z * N_Y + lax.rem(y + i, N_Y),
            t,
        )

    def y_pieces(k, g, to_y):
        lo, w, _ = chunks[k]
        for n, d in enumerate(FWD_GROUPS[g]):
            for c in range(2):
                index = jnp.maximum(met_s[to_y, up(d), 0, c * n_dp + me], 0)
                yield n, c, share[index, :, lo : lo + w]

    def y_build(k, g):
        for i in range(1, N_Y):
            for n, c, piece in y_pieces(k, g, lax.rem(y + i, N_Y)):
                b["y_out"][k][g][i - 1, n, c] = piece
            y_copy(k, g, i, y).start()
        for n, c, piece in y_pieces(k, g, y):
            b["cand"][k][g][y, n, c] = piece

    def ring_copy(k, s, up_way, forward):
        rings, first, ss, rs = (
            (b["ring"], b["first"], b["ring_send"], b["ring_recv"])
            if forward
            else (b["back"], b["lists"], b["back_send"], b["back_recv"])
        )
        from_up = up_way if forward else not up_way
        rows = pl.ds(0 if from_up else side, side)
        src = first[k] if s == 1 else ring_slot(rings, k, s - 1)
        return send_to(
            src.at[rows],
            ring_slot(rings, k, s).at[rows],
            ss.at[k, s, 0 if up_way else 1],
            rs.at[k, s, 0 if up_way else 1],
            up(1 if up_way else N_Z - 1) * N_Y + y,
            t,
        )

    def ring_slot(rings, k, s):
        pair, at = {1: (0, 0), 2: (1, 0), 6: (1, 1), 3: (2, 0), 5: (2, 1), 4: (3, 0)}[s]
        return rings[k][pair].at[at]

    def merge(k, buf, dist, fresh):
        for down in range(2):
            d = (N_Z - dist) % N_Z if down else dist
            g, n = find_group(FWD_GROUPS, d)
            cand = b["cand"][k][g]
            asker = up(d)

            def one(j, carry, down=down, cand=cand, asker=asker, n=n):
                slot = down * side + j
                code = met_s[y, asker, 1, slot]
                mine = cand[lax.rem(lax.div(code, 2), N_Y), n, lax.rem(code, 2)]
                if not fresh:
                    here = lax.div(code, 2 * N_Y) == z
                    mine = jnp.where(here, mine, buf[slot])
                buf[slot] = mine
                return carry

            lax.fori_loop(0, side, one, 0)

    def t_copy(src, owner_t, r0, nr, lo, w, ss, rs, to_t):
        return send_to(
            src, b["nb"].at[pl.ds(r0, nr), pl.ds(owner_t * ts, ts), pl.ds(lo, w)], ss, rs, me, to_t
        )

    def gather_x(u, r0, nr, lo, w, i, from_t):
        return t_copy(
            b["sel"].at[pl.ds(r0, nr), :, pl.ds(lo, w)],
            from_t,
            r0,
            nr,
            lo,
            w,
            b["gx_send"].at[u, i],
            b["gx_recv"].at[u, i],
            lax.rem(x + i, n_x) * 2 + core,
        )

    def gather_mate(u, r0, nr, lo, w, i, from_core):
        from_t = lax.rem(x + n_x - i, n_x) * 2 + from_core
        src = (
            b["sel"].at[pl.ds(r0, nr), :, pl.ds(lo, w)]
            if i == 0
            else b["nb"].at[pl.ds(r0, nr), pl.ds(from_t * ts, ts), pl.ds(lo, w)]
        )
        return t_copy(
            src, from_t, r0, nr, lo, w, b["gm_send"].at[u, i], b["gm_recv"].at[u, i], mate
        )

    def gather_start(u, r0, nr, lo, w):
        for i in range(1, n_x):
            gather_x(u, r0, nr, lo, w, i, t).start()
        gather_mate(u, r0, nr, lo, w, 0, core).start()

    def gather_forward(u, r0, nr, lo, w):
        for i in range(1, n_x):
            gather_x(u, r0, nr, lo, w, i, lax.rem(x + n_x - i, n_x) * 2 + core).wait_recv()
            gather_mate(u, r0, nr, lo, w, i, core).start()

    def gather_arrived(u, r0, nr, lo, w):
        for i in range(n_x):
            gather_mate(u, r0, nr, lo, w, i, 1 - core).wait_recv()

    def gather_sent(u, r0, nr, lo, w):
        for i in range(n_x):
            if i > 0:
                gather_x(u, r0, nr, lo, w, i, t).wait_send()
            gather_mate(u, r0, nr, lo, w, i, core).wait_send()

    unit_a = (spans, 0, n_req, *halves[0])

    def unit_b(c):
        return (c, 2 * c, 2, *halves[1])

    order = ring_order(chunks, HOPS + 1)
    needs = []
    for s, k in order:
        for d in (HOPS + 1 - s, (N_Z - HOPS - 1 + s) % N_Z):
            pair = (k, find_group(FWD_GROUPS, d)[0])
            if pair not in needs:
                needs.append(pair)
    built, landed = 0, []
    finals = [0, 0]
    for at, (s, k) in enumerate(order):
        dist = HOPS + 1 - s
        wanted = []
        for s2, k2 in order[at : at + 1 + AHEAD]:
            wanted.append((k2, find_group(FWD_GROUPS, HOPS + 1 - s2)[0]))
        while any(pair in needs[built:] for pair in wanted):
            y_build(*needs[built])
            built += 1
        if s > 1:
            for up_way in (True, False):
                ring_copy(k, s - 1, up_way, True).wait_recv()
        g = find_group(FWD_GROUPS, dist)[0]
        if (k, g) not in landed:
            for i in range(1, N_Y):
                y_copy(k, g, i, lax.rem(y + N_Y - i, N_Y)).wait_recv()
            landed.append((k, g))
        buf = b["first"][k] if s == 1 else ring_slot(b["ring"], k, s - 1)
        merge(k, buf, dist, s == 1)
        if s <= HOPS:
            for up_way in (True, False):
                ring_copy(k, s, up_way, True).start()
            continue
        lo, w, half = chunks[k]
        for r in range(n_req):
            b["sel"][r, :, lo : lo + w] = buf[ranks[r]]
        finals[half] += 1
        if finals[half] == sum(1 for c in chunks if c[2] == half):
            if half == 0:
                gather_start(*unit_a)
            else:
                for c in range(spans):
                    gather_start(*unit_b(c))
    b["nb"][:, pl.ds(pl.multiple_of(t * ts, ts), ts), :] = b["sel"][...]

    back_order = [d for members in BWD_GROUPS for d in members]
    per = LANES // ts
    lane_tok = lax.rem(lane, ts)
    lane_piece = lax.div(lane, ts)
    tall = lax.broadcasted_iota(jnp.int32, (b["place"].shape[0], LANES), 0)
    for group in range(b["place"].shape[1] // LANES):
        line = jnp.full((1, LANES), -1, jnp.int32)
        for j in range(per):
            piece = group * per + j
            c, pos, from_y = piece % 2, piece // 2 % N_Z, piece // 2 // N_Z
            slab = met_s[from_y, up(back_order[pos]), 0, c * n_dp + me]
            line = jnp.where(lane_piece == j, slab * ts + lane_tok, line)
        b["place"][:, group * LANES : (group + 1) * LANES] = jnp.where(
            tall == line, 1.0, 0.0
        ).astype(bf16)

    for load in loads[1:]:
        load.wait()
    gather_forward(*unit_a)
    gather_forward(*unit_b(0))
    gather_arrived(*unit_a)

    def mate_copy(c):
        rows = pl.ds(2 * c, 2)
        return send_to(
            b["dn"].at[1 - core, :, rows],
            b["from_mate"].at[:, rows],
            b["rm_send"].at[c],
            b["rm_recv"].at[c],
            me,
            mate,
        )

    def x_copy(u, r0, nr, half, i):
        lo, w = halves[half]
        to_x = lax.rem(x + i, n_x)
        return send_to(
            b["chip"].at[to_x, pl.ds(r0, nr), :, pl.ds(lo, w)],
            b["from_x"].at[i - 1, pl.ds(r0, nr), :, pl.ds(lo, w)],
            b["rx_send"].at[u, i],
            b["rx_recv"].at[u, i],
            me,
            to_x * 2 + core,
        )

    def pair_sum(c):
        mate_copy(c).wait_recv()
        rows = pl.ds(2 * c, 2)
        both = b["dn"][core, :, rows].astype(jnp.float32) + b["from_mate"][:, rows].astype(jnp.float32)
        b["chip"][:, rows] = both.astype(bf16)
        for i in range(1, n_x):
            x_copy(c, 2 * c, 2, 0, i).start()

    def span(c, carry):
        @pl.when(c + 1 < spans)
        def _():
            gather_forward(*unit_b(c + 1))

        gather_arrived(*unit_b(c))
        tokens = pl.ds(pl.multiple_of(c * SPAN, SPAN), SPAN)
        rows = b["nb"][pl.ds(2 * c, 2)].reshape(2 * n_tokens, enc)
        att_c, dq_c, dn_c = span_grads(
            b["q"][tokens, :], b["g"][tokens, :], rows, b["wk"][...], b["wv"][...]
        )
        b["att_v"][tokens, :] = att_c
        b["dq_v"][tokens, :] = dq_c
        for rr in range(2):
            for to_t in range(n_tp):
                lo = rr * n_tokens + to_t * ts
                b["dn"][to_t % 2, to_t // 2, 2 * c + rr] = dn_c[lo : lo + ts]
        mate_copy(c).start()

        @pl.when(c >= 1)
        def _():
            pair_sum(c - 1)

        return carry

    lax.fori_loop(0, spans, span, 0)
    stores = [
        pltpu.make_async_copy(b["att_v"], att, b["load_sem"].at[6]),
        pltpu.make_async_copy(b["dq_v"], dq, b["load_sem"].at[7]),
    ]
    for store in stores:
        store.start()
    pair_sum(spans - 1)
    for i in range(1, n_x):
        x_copy(spans, 0, n_req, 1, i).start()

    def back_lists(half):
        lo, w = halves[half]
        if half == 0:

            def landed_x(c, carry):
                for i in range(1, n_x):
                    x_copy(c, 2 * c, 2, 0, i).wait_recv()
                return carry

            lax.fori_loop(0, spans, landed_x, 0)
        else:
            for i in range(1, n_x):
                x_copy(spans, 0, n_req, 1, i).wait_recv()

        def add(j, carry):
            total = b["chip"][x, j, :, lo : lo + w].astype(jnp.float32)
            for i in range(1, n_x):
                total = total + b["from_x"][i - 1, j, :, lo : lo + w].astype(jnp.float32)
            b["total"][half][j] = total.astype(bf16)
            return carry

        lax.fori_loop(0, n_req, add, 0)
        for k, (k_lo, k_w, k_half) in enumerate(chunks):
            if k_half == half:

                def pick(j, carry, k=k, at=k_lo - lo, k_w=k_w):
                    b["lists"][k][j] = b["total"][half][met_s[y, z, 1, n_req + j], :, at : at + k_w]
                    return carry

                lax.fori_loop(0, n_req, pick, 0)

    def yb_copy(k, h, i, from_y):
        at = sum(len(m) for m in BWD_GROUPS[:h])
        return send_to(
            b["yb_out"][k][h].at[i - 1],
            b["got"][k].at[from_y, pl.ds(at, len(BWD_GROUPS[h]))],
            b["yb_send"].at[k, h, i],
            b["yb_recv"].at[k, h, i],
            z * N_Y + lax.rem(y + i, N_Y),
            t,
        )

    def yb_pieces(k, h, to_y):
        for n, d in enumerate(BWD_GROUPS[h]):
            for c in range(2):
                j = met_s[y, up(d), 0, (2 + c) * n_dp + z * N_Y + to_y]
                j = jnp.minimum(jnp.maximum(j, 0), n_req - 1)
                if d == 0:
                    piece = b["lists"][k][j]
                elif d in (1, 7, 4):
                    piece = b["back"][k][0 if d != 4 else 3][0, j]
                else:
                    early = jnp.where(j < side, d, N_Z - d) < 4
                    piece = b["back"][k][1 if d in (2, 6) else 2][jnp.where(early, 0, 1), j]
                yield n, c, piece

    def yb_build(k, h):
        at = sum(len(m) for m in BWD_GROUPS[:h])
        for i in range(1, N_Y):
            for n, c, piece in yb_pieces(k, h, lax.rem(y + i, N_Y)):
                b["yb_out"][k][h][i - 1, n, c] = piece
            yb_copy(k, h, i, y).start()
        for n, c, piece in yb_pieces(k, h, y):
            b["got"][k][y, at + n, c] = piece

    listed = [False, False]
    for s, k in ring_order(chunks, HOPS + 1):
        half = chunks[k][2]
        if not listed[half]:
            back_lists(half)
            listed[half] = True
        if s > 1:
            for up_way in (True, False):
                ring_copy(k, s - 1, up_way, False).wait_recv()
        if s <= HOPS:
            for up_way in (True, False):
                ring_copy(k, s, up_way, False).start()
        if s - 1 in BWD_READY:
            yb_build(k, BWD_READY[s - 1])

    for k, (lo, w, _) in enumerate(chunks):
        for h in range(len(BWD_GROUPS)):
            for i in range(1, N_Y):
                yb_copy(k, h, i, lax.rem(y + N_Y - i, N_Y)).wait_recv()
        pieces = b["got"][k][...].reshape(b["place"].shape[1], w)
        dt[:, :, lo : lo + w] = nn(b["place"][...], pieces).reshape(dt.shape[0], ts, w)

    for store in stores:
        store.wait()
    for k in range(nk):
        for g in range(len(FWD_GROUPS)):
            for i in range(1, N_Y):
                y_copy(k, g, i, y).wait_send()
                yb_copy(k, g, i, y).wait_send()
        for s in range(1, HOPS + 1):
            for up_way in (True, False):
                ring_copy(k, s, up_way, True).wait_send()
                ring_copy(k, s, up_way, False).wait_send()
    gather_sent(*unit_a)
    for i in range(1, n_x):
        x_copy(spans, 0, n_req, 1, i).wait_send()

    def drain(c, carry):
        gather_sent(*unit_b(c))
        mate_copy(c).wait_send()
        for i in range(1, n_x):
            x_copy(c, 2 * c, 2, 0, i).wait_send()
        return carry

    lax.fori_loop(0, spans, drain, 0)


def on_device(queries, cotangent, table, key_weight, value_weight, owners, slots):
    n_dp = lax.axis_size("dp")
    n_tp = lax.axis_size("tensor")
    n_slabs, n_tokens, enc = table.shape
    ts = n_tokens // n_tp
    spans = owners.shape[0]
    n_req = 2 * spans
    n_x = n_tp // 2
    side = n_req // 2
    chunks = lane_chunks(enc)
    nk = len(chunks)
    first_w = sum(w for _, w, half in chunks if half == 0)
    dma = pltpu.SemaphoreType.DMA
    bf16 = jnp.bfloat16
    vm = lambda *shape: pltpu.VMEM(shape, bf16)
    ng = len(FWD_GROUPS)
    rings = lambda w: [vm(n, n_req, ts, w) for n in (1, 2, 2, 1)]
    scratch = dict(
        share=vm(n_slabs, ts, enc),
        wk=vm(*key_weight.shape),
        wv=vm(*value_weight.shape),
        q=vm(*queries.shape),
        g=vm(*cotangent.shape),
        att_v=vm(*queries.shape),
        dq_v=vm(*queries.shape),
        row=pltpu.VMEM((2, LANES), jnp.int32),
        met=pltpu.VMEM((N_Y, N_Z, 2, LANES), jnp.int32),
        met_s=pltpu.SMEM((N_Y, N_Z, 2, LANES), jnp.int32),
        y_out=[[vm(N_Y - 1, len(m), 2, ts, w) for m in FWD_GROUPS] for _, w, _ in chunks],
        cand=[[vm(N_Y, len(m), 2, ts, w) for m in FWD_GROUPS] for _, w, _ in chunks],
        first=[vm(n_req, ts, w) for _, w, _ in chunks],
        ring=[rings(w) for _, w, _ in chunks],
        sel=vm(n_req, ts, enc),
        nb=vm(n_req, n_tokens, enc),
        place=vm(n_slabs * ts, 2 * n_dp * ts),
        dn=vm(2, n_x, n_req, ts, enc),
        from_mate=vm(n_x, n_req, ts, enc),
        chip=vm(n_x, n_req, ts, enc),
        from_x=vm(max(n_x - 1, 1), n_req, ts, enc),
        total=[vm(n_req, ts, first_w), vm(n_req, ts, enc - first_w)],
        lists=[vm(n_req, ts, w) for _, w, _ in chunks],
        back=[rings(w) for _, w, _ in chunks],
        yb_out=[[vm(N_Y - 1, len(m), 2, ts, w) for m in BWD_GROUPS] for _, w, _ in chunks],
        got=[vm(N_Y, N_Z, 2, ts, w) for _, w, _ in chunks],
        load_sem=dma((8,)),
        meta_send=dma((N_Z + N_Y,)),
        meta_recv=dma((N_Z + N_Y,)),
        y_send=dma((nk, ng, N_Y)),
        y_recv=dma((nk, ng, N_Y)),
        yb_send=dma((nk, ng, N_Y)),
        yb_recv=dma((nk, ng, N_Y)),
        ring_send=dma((nk, HOPS + 1, 2)),
        ring_recv=dma((nk, HOPS + 1, 2)),
        back_send=dma((nk, HOPS + 1, 2)),
        back_recv=dma((nk, HOPS + 1, 2)),
        gx_send=dma((spans + 1, n_x)),
        gx_recv=dma((spans + 1, n_x)),
        gm_send=dma((spans + 1, n_x)),
        gm_recv=dma((spans + 1, n_x)),
        rm_send=dma((spans,)),
        rm_recv=dma((spans,)),
        rx_send=dma((spans + 1, n_x)),
        rx_recv=dma((spans + 1, n_x)),
    )
    leaves, treedef = jax.tree_util.tree_flatten(scratch)
    anywhere = pl.BlockSpec(memory_space=pl.ANY)
    return pl.pallas_call(
        functools.partial(fused_kernel, n_dp, n_tp, treedef),
        out_shape=[
            jax.ShapeDtypeStruct(queries.shape, bf16),
            jax.ShapeDtypeStruct(queries.shape, bf16),
            jax.ShapeDtypeStruct((n_slabs, ts, enc), jnp.float32),
        ],
        in_specs=[pl.BlockSpec(memory_space=pltpu.SMEM)] * 2 + [anywhere] * 5,
        out_specs=[anywhere, anywhere, pl.BlockSpec(memory_space=pltpu.VMEM)],
        scratch_shapes=leaves,
        compiler_params=pltpu.CompilerParams(
            collective_id=0, has_side_effects=True, vmem_limit_bytes=VMEM_LIMIT
        ),
        name="spanned",
    )(owners.T, slots.T, table, queries, cotangent, key_weight, value_weight)


def solution(mesh):
    in_specs = (
        P("dp", "tensor"),
        P("dp", "tensor"),
        P("dp", None, None),
        P(None, "tensor"),
        P(None, "tensor"),
        P("dp", None),
        P("dp", None),
    )
    out_specs = (P("dp", "tensor"), P("dp", "tensor"), P("dp", "tensor", None))
    return jax.shard_map(
        on_device, mesh=mesh, in_specs=in_specs, out_specs=out_specs, check_vma=False
    )
```

time: 650 us -> 159 us (0.24); the launches traced: 639 us -> 158 us
  waiting for transfers between devices: 450 us -> 0 us
  Pallas kernels: 0 us -> 152 us
  matrix products: 71.7 us -> 0 us
  local copies, waits for them, and re-layouts: 64 us -> 5.9 us
  blocking collectives: 21 us -> 0 us
  starting transfers between devices: 15.5 us -> 0 us
  between operations: 14.4 us -> 0.64 us
    all_to_all x2 -> x0, waiting for transfers between devices: 381 us -> none  [the longest x1 320 us: on_device(): lax.all_to_all(sent_rows, 'dp', split_axis=0, concat_axis=0, tiled=True)]
    pallas_call x0 -> x1, Pallas kernels: none -> 152 us  [on_device(): pl.pallas_call(functools.partial(fused_kernel, n_dp, n_tp, treedef), out_...]
    dot_general x9 -> x0, matrix products: 71.7 us -> none  [the longest x1 17.2 us: on_device(): jnp.einsum('chqk,cqhd->ckhd', dscores, query_heads, preferred_element_typ...]
    reduce_scatter x1 -> x0, waiting for transfers between devices: 68.9 us -> none  [on_device(): lax.psum_scatter(summed.reshape(tok_share * lax.axis_size('tensor'), n_re...]
    all_to_all x1 -> x0, blocking collectives: 21 us -> none  [on_device(): lax.all_to_all(request_buffer.reshape(n_dp, capacity), 'dp', split_axis=0...]
    concatenate x5 -> x0, local copies, waits for them, and re-layouts: 18.5 us -> none  [the longest x4 17.4 us: on_device(): jnp.concatenate([d_keys.reshape(spans, 2 * n_tokens, kv_width), d_values....]
    gather x2 -> x0, local copies, waits for them, and re-layouts: 17.9 us -> none  [the longest x1 9.97 us: on_device(): sent_rows = table[safe_slot]]
    all_to_all x2 -> x0, starting transfers between devices: 15.4 us -> none  [the longest x1 10.2 us: on_device(): lax.all_to_all(back_buffer.reshape(n_dp, capacity, tok_share, enc_width),...]
  transfers between devices with their start and end apart: 3 -> 0, of which waited for: 3 -> 0; matrix products, arithmetic and copies ran while one was open for 4% -> 0% of each run, Pallas kernels for 0% -> 0%
where the time goes in v2:
time: 159 us; the launch traced here: 158 us
  Pallas kernels  152 us (96%)
  local copies, waits for them, and re-layouts  5.9 us (4%)
    pallas_call x1, Pallas kernels, on_device(): pl.pallas_call(functools.partial(fused_kernel, n_dp, n_tp, treedef), out_...  152 us
    unnamed x3, local copies, waits for them, and re-layouts  5.9 us

profile of v2, /device:TPU:6, one launch (start us, length us, event | category | flops | bytes accessed | tf_op | source)
XLA Modules:
  0.0 158.3 jit_solution(11561905526449987595)
XLA Ops:
  0.6 151.8 %spanned.1 = (bf16[512,512]{1,0:T(8,128)(2,1)}, bf16[512,512]{1,0:T(8,128)(2,1)}, f32[16,16,896]{2,1,0:T(8,128)}) custom-call(s32[2,8]{1,0:T(2,128)} %bitcast.2, s32[2,8]{1,0:T(2,128)} %bitcast.3, bf16[16,128,896]{2,1,0:T(8,128)(2,1)} %table.1, bf16[512,512]{1,0:T(8,128)(2,1)} %queries.1, bf16[512,512]{1,0:T(8,128)(2,1)} %cotangent.1, ...), custom_call_target="tpu_custom_call" | custom-call | tf_op jit(solution)/shard_map/spanned/pallas_call | solution.py:636
  152.4 1.9 %copy.13 = bf16[512,512]{1,0:T(8,128)(2,1)} copy(bf16[512,512]{1,0:T(8,128)(2,1)} %get-tuple-element.6) | data formatting | bytes 1048576
  154.3 1.9 %copy.14 = bf16[512,512]{1,0:T(8,128)(2,1)} copy(bf16[512,512]{1,0:T(8,128)(2,1)} %get-tuple-element.7) | data formatting | bytes 1048576
  156.2 2.2 %copy.15 = f32[16,16,896]{2,1,0:T(8,128)} copy(f32[16,16,896]{2,1,0:T(8,128)} %get-tuple-element.8) | data formatting | bytes 1835008

commit v3 on v2

v3 whole, which is shorter than its diff:
```python
import functools
import math

import jax
import jax.numpy as jnp
from jax import lax
from jax.experimental import pallas as pl
from jax.experimental.pallas import tpu as pltpu
from jax.sharding import PartitionSpec as P

HD = 128
SPAN = 64
LANES = 128
N_Y = 4
N_Z = 8
HOPS = 6
N_X = 4
CHUNKS = 4
AHEAD = 4
GATHER_AHEAD = 8
PASS_AHEAD = 4
FAR_AHEAD = 2
FWD_GROUPS = ((6, 2), (5, 3), (4,), (1, 7, 0))
BWD_GROUPS = ((0, 1, 7), (4,), (3, 5), (2, 6))
BWD_READY = {1: 0, 4: 1, 5: 2, 6: 3}
MESH = pl.DeviceIdType.MESH
VMEM_LIMIT = 56 * 1024 * 1024


def lane_chunks(enc):
    units = enc // LANES
    count = min(CHUNKS, units)
    chunks = []
    at = 0
    for left in range(count, 0, -1):
        n = (units - at) // left
        chunks.append((at * LANES, n * LANES))
        at += n
    return chunks


def ring_order(chunks, last, backward):
    ks = range(len(chunks))
    return [(s, k) for s in range(1, last + 1) for k in (reversed(ks) if backward else ks)]


def find_group(groups, d):
    for g, members in enumerate(groups):
        if d in members:
            return g, members.index(d)


def nt(a, b):
    return lax.dot_general(a, b, (((1,), (1,)), ((), ())), preferred_element_type=jnp.float32)


def tn(a, b):
    return lax.dot_general(a, b, (((0,), (0,)), ((), ())), preferred_element_type=jnp.float32)


def nn(a, b):
    return lax.dot_general(a, b, (((1,), (0,)), ((), ())), preferred_element_type=jnp.float32)


def span_grads(q, g, rows, wk, wv):
    bf16 = jnp.bfloat16
    scale = 1.0 / math.sqrt(HD)
    heads = q.shape[1] // HD
    keys = nn(rows, wk).astype(bf16)
    values = nn(rows, wv).astype(bf16)
    cut = [slice(h * HD, (h + 1) * HD) for h in range(heads)]
    scores = jnp.concatenate([nt(q[:, s], keys[:, s]) for s in cut], axis=0) * scale
    d_weights = jnp.concatenate([nt(g[:, s], values[:, s]) for s in cut], axis=0)
    e = jnp.exp(scores - jnp.max(scores, axis=1, keepdims=True))
    probs = e / jnp.sum(e, axis=1, keepdims=True)
    row_sums = jnp.sum(d_weights * probs, axis=1, keepdims=True)
    ds = (probs * (d_weights - row_sums) * scale).astype(bf16)
    weights = probs.astype(bf16)
    attended, d_query, d_keys, d_values = [], [], [], []
    for h, s in enumerate(cut):
        w_h = weights[h * SPAN : (h + 1) * SPAN]
        ds_h = ds[h * SPAN : (h + 1) * SPAN]
        attended.append(nn(w_h, values[:, s]).astype(bf16))
        d_query.append(nn(ds_h, keys[:, s]).astype(bf16))
        d_keys.append(tn(ds_h, q[:, s]).astype(bf16))
        d_values.append(tn(w_h, g[:, s]).astype(bf16))
    dn = nt(jnp.concatenate(d_keys, axis=1), wk) + nt(jnp.concatenate(d_values, axis=1), wv)
    return (
        jnp.concatenate(attended, axis=1),
        jnp.concatenate(d_query, axis=1),
        dn.astype(bf16),
    )


def fused_kernel(
    n_dp, n_tp, treedef, owners, slots, table, queries, cotangent, key_weight, value_weight, att, dq, dt, *flat
):
    b = jax.tree_util.tree_unflatten(treedef, flat)
    bf16 = jnp.bfloat16
    me = lax.axis_index("dp")
    t = lax.axis_index("tensor")
    z, y = lax.div(me, N_Y), lax.rem(me, N_Y)
    x, core = lax.div(t, 2), lax.rem(t, 2)
    mate = x * 2 + 1 - core
    x_up, x_far, x_down = [lax.rem(x + i, N_X) for i in range(1, N_X)]
    n_req, ts, enc = b["sel"].shape
    spans = n_req // 2
    side = n_req // 2
    n_tokens = ts * n_tp
    chunks = lane_chunks(enc)
    nk = len(chunks)

    def up(d):
        return lax.rem(z + d, N_Z)

    def send_to(src, dst, ss, rs, dp_to, t_to):
        return pltpu.make_async_remote_copy(
            src_ref=src, dst_ref=dst, send_sem=ss, recv_sem=rs, device_id=(dp_to, t_to), device_id_type=MESH
        )

    def landed_all(ref, sem):
        pltpu.make_async_copy(ref, ref, sem).wait()

    loads = [
        pltpu.make_async_copy(table.at[:, pl.ds(t * ts, ts), :], b["share"], b["load_sem"].at[0]),
        pltpu.make_async_copy(key_weight, b["wk"], b["load_sem"].at[1]),
        pltpu.make_async_copy(value_weight, b["wv"], b["load_sem"].at[2]),
        pltpu.make_async_copy(queries, b["q"], b["load_sem"].at[3]),
        pltpu.make_async_copy(cotangent, b["g"], b["load_sem"].at[4]),
    ]
    for load in loads:
        load.start()

    barrier = pltpu.get_barrier_semaphore()
    def hello(i, carry):
        pl.semaphore_signal(
            barrier, inc=1, device_id=(lax.rem(me + i, n_dp), t), device_id_type=MESH
        )
        return carry

    lax.fori_loop(1, n_dp, hello, 0)
    for peer_t in (x_up * 2 + core, x_down * 2 + core, mate):
        pl.semaphore_signal(barrier, inc=1, device_id=(me, peer_t), device_id_type=MESH)

    lane = lax.broadcasted_iota(jnp.int32, (1, LANES), 1)
    lane_dp = lane & (n_dp - 1)
    lane_place = lax.shift_right_logical(lane, int(math.log2(n_dp))) & 1
    is_slot = lane < 2 * n_dp
    own = [owners[r % 2, r // 2] for r in range(n_req)]
    far = [lax.rem(z - lax.div(own[r], N_Y) + N_Z, N_Z) for r in range(n_req)]
    key = [jnp.where(far[r] == 0, N_Z // 2, far[r]) for r in range(n_req)]
    asked_row = jnp.full((1, LANES), -1, jnp.int32)
    list_row = jnp.zeros((1, LANES), jnp.int32)
    seen = jnp.zeros((1, LANES), jnp.int32)
    ranks = []
    for r in range(n_req):
        before = jnp.int32(0)
        rank = jnp.int32(0)
        for other in range(n_req):
            if other < r:
                before = before + jnp.where(own[other] == own[r], 1, 0)
                rank = rank + jnp.where(key[other] <= key[r], 1, 0)
            elif other > r:
                rank = rank + jnp.where(key[other] < key[r], 1, 0)
        ranks.append(rank)
        hit = lane_dp == own[r]
        asked_row = jnp.where(
            hit & (seen == lane_place), jnp.where(is_slot, slots[r % 2, r // 2], rank), asked_row
        )
        seen = seen + hit.astype(jnp.int32)
        list_row = jnp.where(lane == rank, 2 * own[r] + before, list_row)
        list_row = jnp.where(lane == rank + n_req, r, list_row)
    my_rows = jnp.concatenate([asked_row, list_row], axis=0)
    b["row"][...] = my_rows

    pl.semaphore_wait(barrier, n_dp - 1 + 3)

    met, met_s = b["met"], b["met_s"]

    def ask(i, carry):
        send_to(
            b["row"], met.at[me], b["meta_send"], b["meta_recv"], lax.rem(me + i, n_dp), t
        ).start()
        return carry

    lax.fori_loop(1, n_dp, ask, 0)
    met[me] = my_rows
    others = met.at[pl.ds(0, n_dp - 1)]
    landed_all(others, b["meta_recv"])
    to_smem = pltpu.make_async_copy(met, met_s, b["load_sem"].at[5])
    loads[0].wait()
    to_smem.start()
    to_smem.wait()

    share = b["share"]

    def y_copy(k, g, i, from_y):
        return send_to(
            b["y_out"][k][g].at[i - 1],
            b["cand"][k][g].at[from_y],
            b["y_send"].at[k, g],
            b["y_recv"].at[k, g],
            z * N_Y + lax.rem(y + i, N_Y),
            t,
        )

    def y_pieces(k, g, to_y):
        lo, w = chunks[k]
        for n, d in enumerate(FWD_GROUPS[g]):
            for c in range(2):
                index = jnp.maximum(met_s[up(d) * N_Y + to_y, 0, c * n_dp + me], 0)
                yield n, c, share[index, :, lo : lo + w]

    def y_build(k, g):
        for i in range(1, N_Y):
            for n, c, piece in y_pieces(k, g, lax.rem(y + i, N_Y)):
                b["y_out"][k][g][i - 1, n, c] = piece
            y_copy(k, g, i, y).start()
        for n, c, piece in y_pieces(k, g, y):
            b["cand"][k][g][y, n, c] = piece

    def ring_copy(k, s, up_way, forward):
        rings, first, ss, rs = (
            (b["ring"], b["first"], b["ring_send"], b["ring_recv"])
            if forward
            else (b["back"], b["lists"], b["back_send"], b["back_recv"])
        )
        from_up = up_way if forward else not up_way
        rows = pl.ds(0 if from_up else side, side)
        src = first[k] if s == 1 else ring_slot(rings, k, s - 1)
        return send_to(
            src.at[rows],
            ring_slot(rings, k, s).at[rows],
            ss.at[k, 0 if up_way else 1],
            rs.at[k, s - 1],
            up(1 if up_way else N_Z - 1) * N_Y + y,
            t,
        )

    def ring_slot(rings, k, s):
        pair, at = {1: (0, 0), 2: (1, 0), 6: (1, 1), 3: (2, 0), 5: (2, 1), 4: (3, 0)}[s]
        return rings[k][pair].at[at]

    def merge(k, buf, dist, fresh):
        for down in range(2):
            d = (N_Z - dist) % N_Z if down else dist
            g, n = find_group(FWD_GROUPS, d)
            cand = b["cand"][k][g]
            asker = up(d)

            def one(j, carry, down=down, cand=cand, asker=asker, n=n):
                slot = down * side + j
                code = met_s[asker * N_Y + y, 1, slot]
                mine = cand[lax.rem(lax.div(code, 2), N_Y), n, lax.rem(code, 2)]
                if not fresh:
                    here = lax.div(code, 2 * N_Y) == z
                    mine = jnp.where(here, mine, buf[slot])
                buf[slot] = mine
                return carry

            lax.fori_loop(0, side, one, 0)

    def share_of(owner_t, row, n):
        return b["nb"].at[pl.ds(row, n), pl.ds(owner_t * ts, ts)]

    def gather_start(c, lo, w):
        own_rows = b["sel"].at[pl.ds(2 * c, 2), :, pl.ds(lo, w)]
        there = b["nb"].at[pl.ds(2 * c, 2), pl.ds(t * ts, ts), pl.ds(lo, w)]
        for to_x in (x_up, x_down):
            send_to(
                own_rows, there, b["gx_send"].at[c], b["gx_recv"].at[c], me, to_x * 2 + core
            ).start()
        send_to(own_rows, there, b["gm_send"].at[c], b["gm_recv"].at[c], me, mate).start()

    def gather_pass(c):
        landed_all(b["nb"].at[pl.ds(2 * c, 2), pl.ds(0, 2 * ts)], b["gx_recv"].at[c])
        for from_x, to_x, way in ((x_down, x_up, 0), (x_up, x_down, 1)):
            one = share_of(from_x * 2 + core, 2 * c + way, 1)
            send_to(
                one, one, b["gf_send"].at[c], b["gf_recv"].at[c], me, to_x * 2 + core
            ).start()
        for from_x in (x_down, x_up):
            near = share_of(from_x * 2 + core, 2 * c, 2)
            send_to(near, near, b["gm_send"].at[c], b["gm_recv"].at[c], me, mate).start()

    def gather_far(c):
        far_share = share_of(x_far * 2 + core, 2 * c, 2)
        landed_all(far_share, b["gf_recv"].at[c])
        send_to(far_share, far_share, b["gm_send"].at[c], b["gm_recv"].at[c], me, mate).start()

    def gather_arrived(c):
        landed_all(
            b["nb"].at[pl.ds(2 * c, 2), pl.ds(0, N_X * ts)], b["gm_recv"].at[c]
        )

    def gather_sent(c):
        landed_all(b["nb"].at[pl.ds(2 * c, 2), pl.ds(0, 2 * ts)], b["gx_send"].at[c])
        landed_all(b["sel"].at[pl.ds(2 * c, 2)], b["gf_send"].at[c])
        landed_all(b["nb"].at[pl.ds(2 * c, 2), pl.ds(0, N_X * ts)], b["gm_send"].at[c])

    order = ring_order(chunks, HOPS + 1, False)
    needs = []
    for s, k in order:
        for d in (HOPS + 1 - s, (N_Z - HOPS - 1 + s) % N_Z):
            pair = (k, find_group(FWD_GROUPS, d)[0])
            if pair not in needs:
                needs.append(pair)
    built, landed = 0, []
    for at, (s, k) in enumerate(order):
        dist = HOPS + 1 - s
        wanted = []
        for s2, k2 in order[at : at + 1 + AHEAD]:
            wanted.append((k2, find_group(FWD_GROUPS, HOPS + 1 - s2)[0]))
        while any(pair in needs[built:] for pair in wanted):
            y_build(*needs[built])
            built += 1
        if s > 1:
            landed_all(ring_slot(b["ring"], k, s - 1), b["ring_recv"].at[k, s - 2])
        g = find_group(FWD_GROUPS, dist)[0]
        if (k, g) not in landed:
            landed_all(b["cand"][k][g].at[pl.ds(0, N_Y - 1)], b["y_recv"].at[k, g])
            landed.append((k, g))
        buf = b["first"][k] if s == 1 else ring_slot(b["ring"], k, s - 1)
        merge(k, buf, dist, s == 1)
        if s <= HOPS:
            for up_way in (True, False):
                if s > 1:
                    ring_copy(k, s - 1, up_way, True).wait_send()
                ring_copy(k, s, up_way, True).start()
            continue
        lo, w = chunks[k]
        for r in range(n_req):
            b["sel"][r, :, lo : lo + w] = buf[ranks[r]]
        for c in range(min(GATHER_AHEAD, spans)):
            gather_start(c, lo, w)
    b["nb"][:, pl.ds(pl.multiple_of(t * ts, ts), ts), :] = b["sel"][...]

    back_order = [d for members in BWD_GROUPS for d in members]
    per = LANES // ts
    lane_tok = lax.rem(lane, ts)
    lane_piece = lax.div(lane, ts)
    tall = lax.broadcasted_iota(jnp.int32, (b["place"].shape[0], LANES), 0)
    for group in range(b["place"].shape[1] // LANES):
        line = jnp.full((1, LANES), -1, jnp.int32)
        for j in range(per):
            piece = group * per + j
            c, pos, from_y = piece % 2, piece // 2 % N_Z, piece // 2 // N_Z
            slab = met_s[up(back_order[pos]) * N_Y + from_y, 0, c * n_dp + me]
            line = jnp.where(lane_piece == j, slab * ts + lane_tok, line)
        b["place"][:, group * LANES : (group + 1) * LANES] = jnp.where(
            tall == line, 1.0, 0.0
        ).astype(bf16)

    for load in loads[1:]:
        load.wait()
    for c in range(min(PASS_AHEAD, spans)):
        gather_pass(c)
    for c in range(min(FAR_AHEAD, spans)):
        gather_far(c)

    def mate_copy(c):
        rows = pl.ds(2 * c, 2)
        return send_to(
            b["dn"].at[1 - core, :, rows],
            b["from_mate"].at[:, rows],
            b["rm_send"].at[c],
            b["rm_recv"].at[c],
            me,
            mate,
        )

    def rows_to(to_x, src, dst, ss, rs):
        return send_to(src, dst, ss, rs, me, to_x * 2 + core)

    def far_copy(c, way):
        row = pl.ds(2 * c + way, 1)
        return rows_to(
            x_down if way else x_up,
            b["chip"].at[x_far, row],
            b["from_far"].at[way, pl.ds(c, 1)],
            b["rf_send"].at[c],
            b["rf_recv"].at[c],
        )

    def near_copy(c, way):
        rows = pl.ds(2 * c, 2)
        to_x = x_down if way else x_up
        return rows_to(
            to_x,
            b["chip"].at[to_x, rows],
            b["from_near"].at[way, rows],
            b["rn_send"].at[c],
            b["rn_recv"].at[c],
        )

    def pair_sum(c):
        mate_copy(c).wait_recv()
        rows = pl.ds(2 * c, 2)
        both = b["dn"][core, :, rows].astype(jnp.float32) + b["from_mate"][:, rows].astype(jnp.float32)
        b["chip"][:, rows] = both.astype(bf16)
        for way in range(2):
            far_copy(c, way).start()

    def near_sum(c):
        landed_all(b["from_far"].at[:, pl.ds(c, 1)], b["rf_recv"].at[c])
        for way in range(2):
            to_x, row = x_down if way else x_up, 2 * c + way
            both = b["chip"][to_x, row].astype(jnp.float32) + b["from_far"][way, c].astype(jnp.float32)
            b["chip"][to_x, row] = both.astype(bf16)
            near_copy(c, way).start()

    def last_sum(c):
        rows = pl.ds(2 * c, 2)
        total = b["chip"][x, rows].astype(jnp.float32)
        landed_all(b["from_near"].at[:, rows], b["rn_recv"].at[c])
        for way in range(2):
            total = total + b["from_near"][way, rows].astype(jnp.float32)
        b["total"][rows] = total.astype(bf16)

    def span(c, carry):
        @pl.when(c + GATHER_AHEAD < spans)
        def _():
            gather_start(c + GATHER_AHEAD, 0, enc)

        @pl.when(c + PASS_AHEAD < spans)
        def _():
            gather_pass(c + PASS_AHEAD)

        @pl.when(c + FAR_AHEAD < spans)
        def _():
            gather_far(c + FAR_AHEAD)

        gather_arrived(c)
        tokens = pl.ds(pl.multiple_of(c * SPAN, SPAN), SPAN)
        rows = b["nb"][pl.ds(2 * c, 2)].reshape(2 * n_tokens, enc)
        att_c, dq_c, dn_c = span_grads(
            b["q"][tokens, :], b["g"][tokens, :], rows, b["wk"][...], b["wv"][...]
        )
        b["att_v"][tokens, :] = att_c
        b["dq_v"][tokens, :] = dq_c
        for rr in range(2):
            for to_t in range(n_tp):
                lo = rr * n_tokens + to_t * ts
                b["dn"][to_t % 2, to_t // 2, 2 * c + rr] = dn_c[lo : lo + ts]
        mate_copy(c).start()

        @pl.when(c >= 1)
        def _():
            pair_sum(c - 1)

        @pl.when(c >= 2)
        def _():
            near_sum(c - 2)

        @pl.when(c >= 3)
        def _():
            last_sum(c - 3)

        return carry

    lax.fori_loop(0, spans, span, 0)
    stores = [
        pltpu.make_async_copy(b["att_v"], att, b["load_sem"].at[6]),
        pltpu.make_async_copy(b["dq_v"], dq, b["load_sem"].at[7]),
    ]
    for store in stores:
        store.start()
    pair_sum(spans - 1)
    for c in range(max(spans - 2, 0), spans):
        near_sum(c)
    for c in range(max(spans - 3, 0), spans):
        last_sum(c)

    def yb_copy(k, h, i, from_y):
        at = sum(len(m) for m in BWD_GROUPS[:h])
        return send_to(
            b["yb_out"][k][h].at[i - 1],
            b["got"][k].at[from_y, pl.ds(at, len(BWD_GROUPS[h]))],
            b["yb_send"].at[k, h],
            b["yb_recv"].at[k, h],
            z * N_Y + lax.rem(y + i, N_Y),
            t,
        )

    def yb_pieces(k, h, to_y):
        for n, d in enumerate(BWD_GROUPS[h]):
            for c in range(2):
                j = met_s[up(d) * N_Y + y, 0, (2 + c) * n_dp + z * N_Y + to_y]
                j = jnp.minimum(jnp.maximum(j, 0), n_req - 1)
                if d == 0:
                    piece = b["lists"][k][j]
                elif d in (1, 7, 4):
                    piece = b["back"][k][0 if d != 4 else 3][0, j]
                else:
                    early = jnp.where(j < side, d, N_Z - d) < 4
                    piece = b["back"][k][1 if d in (2, 6) else 2][jnp.where(early, 0, 1), j]
                yield n, c, piece

    def yb_build(k, h):
        at = sum(len(m) for m in BWD_GROUPS[:h])
        for i in range(1, N_Y):
            for n, c, piece in yb_pieces(k, h, lax.rem(y + i, N_Y)):
                b["yb_out"][k][h][i - 1, n, c] = piece
            yb_copy(k, h, i, y).start()
        for n, c, piece in yb_pieces(k, h, y):
            b["got"][k][y, at + n, c] = piece

    for s, k in ring_order(chunks, HOPS + 1, True):
        if s == 1:
            lo, w = chunks[k]
            for j in range(n_req):
                b["lists"][k][j] = b["total"][met_s[me, 1, n_req + j], :, lo : lo + w]
        if s > 1:
            landed_all(ring_slot(b["back"], k, s - 1), b["back_recv"].at[k, s - 2])
        if s <= HOPS:
            for up_way in (True, False):
                if s > 1:
                    ring_copy(k, s - 1, up_way, False).wait_send()
                ring_copy(k, s, up_way, False).start()
        if s - 1 in BWD_READY:
            yb_build(k, BWD_READY[s - 1])

    for k, (lo, w) in enumerate(chunks):
        at = 0
        for h, members in enumerate(BWD_GROUPS):
            landed_all(
                b["got"][k].at[pl.ds(0, N_Y - 1), pl.ds(at, len(members))], b["yb_recv"].at[k, h]
            )
            at += len(members)
        pieces = b["got"][k][...].reshape(b["place"].shape[1], w)
        dt[:, :, lo : lo + w] = nn(b["place"][...], pieces).reshape(dt.shape[0], ts, w)

    for store in stores:
        store.wait()
    landed_all(others, b["meta_send"])
    for k in range(nk):
        for g in range(len(FWD_GROUPS)):
            landed_all(b["y_out"][k][g], b["y_send"].at[k, g])
            landed_all(b["yb_out"][k][g], b["yb_send"].at[k, g])
        for up_way in (True, False):
            ring_copy(k, HOPS, up_way, True).wait_send()
            ring_copy(k, HOPS, up_way, False).wait_send()

    def drain(c, carry):
        gather_sent(c)
        mate_copy(c).wait_send()
        landed_all(b["from_far"].at[:, pl.ds(c, 1)], b["rf_send"].at[c])
        landed_all(b["from_near"].at[:, pl.ds(2 * c, 2)], b["rn_send"].at[c])
        return carry

    lax.fori_loop(0, spans, drain, 0)


def finish_kernel(att_in, dq_in, dt_in, att, dq, dt):
    att[...] = att_in[...]
    dq[...] = dq_in[...]
    dt[...] = dt_in[...]


def finish(*arrays):
    parts = 4

    def spec(a):
        block = (a.shape[0] // parts, *a.shape[1:])
        return pl.BlockSpec(block, lambda i: (i,) + (0,) * (len(block) - 1))

    return pl.pallas_call(
        finish_kernel,
        grid=(parts,),
        out_shape=[jax.ShapeDtypeStruct(a.shape, a.dtype) for a in arrays],
        in_specs=[spec(a) for a in arrays],
        out_specs=[spec(a) for a in arrays],
        name="finish",
    )(*arrays)


def on_device(queries, cotangent, table, key_weight, value_weight, owners, slots):
    n_dp = lax.axis_size("dp")
    n_tp = lax.axis_size("tensor")
    n_slabs, n_tokens, enc = table.shape
    ts = n_tokens // n_tp
    spans = owners.shape[0]
    n_req = 2 * spans
    n_x = n_tp // 2
    chunks = lane_chunks(enc)
    nk = len(chunks)
    dma = pltpu.SemaphoreType.DMA
    bf16 = jnp.bfloat16
    vm = lambda *shape: pltpu.VMEM(shape, bf16)
    ng = len(FWD_GROUPS)
    rings = lambda w: [vm(n, n_req, ts, w) for n in (1, 2, 2, 1)]
    scratch = dict(
        share=vm(n_slabs, ts, enc),
        wk=vm(*key_weight.shape),
        wv=vm(*value_weight.shape),
        q=vm(*queries.shape),
        g=vm(*cotangent.shape),
        att_v=vm(*queries.shape),
        dq_v=vm(*queries.shape),
        row=pltpu.VMEM((2, LANES), jnp.int32),
        met=pltpu.VMEM((n_dp, 2, LANES), jnp.int32),
        met_s=pltpu.SMEM((n_dp, 2, LANES), jnp.int32),
        y_out=[[vm(N_Y - 1, len(m), 2, ts, w) for m in FWD_GROUPS] for _, w in chunks],
        cand=[[vm(N_Y, len(m), 2, ts, w) for m in FWD_GROUPS] for _, w in chunks],
        first=[vm(n_req, ts, w) for _, w in chunks],
        ring=[rings(w) for _, w in chunks],
        sel=vm(n_req, ts, enc),
        nb=vm(n_req, n_tokens, enc),
        place=vm(n_slabs * ts, 2 * n_dp * ts),
        dn=vm(2, n_x, n_req, ts, enc),
        from_mate=vm(n_x, n_req, ts, enc),
        chip=vm(n_x, n_req, ts, enc),
        from_far=vm(2, spans, ts, enc),
        from_near=vm(2, n_req, ts, enc),
        total=vm(n_req, ts, enc),
        lists=[vm(n_req, ts, w) for _, w in chunks],
        back=[rings(w) for _, w in chunks],
        yb_out=[[vm(N_Y - 1, len(m), 2, ts, w) for m in BWD_GROUPS] for _, w in chunks],
        got=[vm(N_Y, N_Z, 2, ts, w) for _, w in chunks],
        load_sem=dma((8,)),
        meta_send=dma,
        meta_recv=dma,
        y_send=dma((nk, ng)),
        y_recv=dma((nk, ng)),
        yb_send=dma((nk, ng)),
        yb_recv=dma((nk, ng)),
        ring_send=dma((nk, 2)),
        ring_recv=dma((nk, HOPS)),
        back_send=dma((nk, 2)),
        back_recv=dma((nk, HOPS)),
        gx_send=dma((spans,)),
        gx_recv=dma((spans,)),
        gf_send=dma((spans,)),
        gf_recv=dma((spans,)),
        gm_send=dma((spans,)),
        gm_recv=dma((spans,)),
        rm_send=dma((spans,)),
        rm_recv=dma((spans,)),
        rf_send=dma((spans,)),
        rf_recv=dma((spans,)),
        rn_send=dma((spans,)),
        rn_recv=dma((spans,)),
    )
    leaves, treedef = jax.tree_util.tree_flatten(scratch)
    anywhere = pl.BlockSpec(memory_space=pl.ANY)
    results = pl.pallas_call(
        functools.partial(fused_kernel, n_dp, n_tp, treedef),
        out_shape=[
            jax.ShapeDtypeStruct(queries.shape, bf16),
            jax.ShapeDtypeStruct(queries.shape, bf16),
            jax.ShapeDtypeStruct((n_slabs, ts, enc), jnp.float32),
        ],
        in_specs=[pl.BlockSpec(memory_space=pltpu.SMEM)] * 2 + [anywhere] * 5,
        out_specs=[anywhere, anywhere, pl.BlockSpec(memory_space=pltpu.VMEM)],
        scratch_shapes=leaves,
        compiler_params=pltpu.CompilerParams(
            collective_id=0, has_side_effects=True, vmem_limit_bytes=VMEM_LIMIT
        ),
        name="spanned",
    )(owners.T, slots.T, table, queries, cotangent, key_weight, value_weight)
    return finish(*results)


def solution(mesh):
    in_specs = (
        P("dp", "tensor"),
        P("dp", "tensor"),
        P("dp", None, None),
        P(None, "tensor"),
        P(None, "tensor"),
        P("dp", None),
        P("dp", None),
    )
    out_specs = (P("dp", "tensor"), P("dp", "tensor"), P("dp", "tensor", None))
    return jax.shard_map(
        on_device, mesh=mesh, in_specs=in_specs, out_specs=out_specs, check_vma=False
    )
```

time: 159 us -> 141 us (0.89)
  Pallas kernels: 152 us -> 140 us
  local copies, waits for them, and re-layouts: 5.9 us -> 0 us
    pallas_call x1, Pallas kernels: 152 us -> 136 us  [on_device(): pl.pallas_call(functools.partial(fused_kernel, n_dp, n_tp, treedef), out_...]
    unnamed x3 -> x0, local copies, waits for them, and re-layouts: 5.9 us -> none
    pallas_call x0 -> x1, Pallas kernels: none -> 3.77 us  [finish(): pl.pallas_call(finish_kernel, grid=(parts,), out_shape=[jax.ShapeDtypeStr...]
where the time goes in v3:
time: 141 us; the launch traced here: 140 us
  Pallas kernels  140 us (99%)
    pallas_call x1, Pallas kernels, on_device(): pl.pallas_call(functools.partial(fused_kernel, n_dp, n_tp, treedef), out_...  136 us
    pallas_call x1, Pallas kernels, finish(): pl.pallas_call(finish_kernel, grid=(parts,), out_shape=[jax.ShapeDtypeStr...  3.77 us

profile of v3, /device:TPU:6, one launch (start us, length us, event | category | flops | bytes accessed | tf_op | source)
XLA Modules:
  0.0 140.3 jit_solution(8384106765746746437)
XLA Ops:
  0.6 135.9 %spanned.1 = (bf16[512,512]{1,0:T(8,128)(2,1)}, bf16[512,512]{1,0:T(8,128)(2,1)}, f32[16,16,896]{2,1,0:T(8,128)}) custom-call(s32[2,8]{1,0:T(2,128)} %bitcast.2, s32[2,8]{1,0:T(2,128)} %bitcast.3, bf16[16,128,896]{2,1,0:T(8,128)(2,1)} %table.1, bf16[512,512]{1,0:T(8,128)(2,1)} %queries.1, bf16[512,512]{1,0:T(8,128)(2,1)} %cotangent.1, ...), custom_call_target="tpu_custom_call" | custom-call | tf_op jit(solution)/shard_map/spanned/pallas_call | solution.py:646
  136.5 3.8 %finish.1 = (bf16[512,512]{1,0:T(8,128)(2,1)}, bf16[512,512]{1,0:T(8,128)(2,1)}, f32[16,16,896]{2,1,0:T(8,128)}) custom-call(bf16[512,512]{1,0:T(8,128)(2,1)} %get-tuple-element.6.att_in, bf16[512,512]{1,0:T(8,128)(2,1)} %get-tuple-element.7.dq_in, f32[16,16,896]{2,1,0:T(8,128)} %get-tuple-element.8.dt_in), custom_call_target="tpu_custom_call" | custom-call | tf_op jit(solution)/shard_map/finish/pallas_call | solution.py:567

commit v4 on v3

v4 whole, which is shorter than its diff:
```python
import functools
import math
import types

import jax
import jax.numpy as jnp
from jax import lax
from jax.experimental import pallas as pl
from jax.experimental.pallas import tpu as pltpu
from jax.sharding import PartitionSpec as P

HD = 128
SPAN = 64
LANES = 128
N_Y = 4
N_Z = 8
HOPS = 4
N_X = 4
FAR_SLOTS = 4
WAVES = 2
CHUNKS = 3
AHEAD = 4
FWD_GROUPS = ((4,), (3, 5), (2, 6), (1, 7, 0))
BWD_GROUPS = ((0, 1, 7), (2, 6), (3, 5), (4,))
MESH = pl.DeviceIdType.MESH
VMEM_LIMIT = 56 * 1024 * 1024


def lane_chunks(enc):
    units = enc // LANES
    count = min(CHUNKS, units)
    chunks = []
    at = 0
    for left in range(count, 0, -1):
        n = (units - at) // left
        chunks.append((at * LANES, n * LANES))
        at += n
    return chunks


def find_group(groups, d):
    for g, members in enumerate(groups):
        if d in members:
            return g, members.index(d)


def nt(a, b):
    return lax.dot_general(a, b, (((1,), (1,)), ((), ())), preferred_element_type=jnp.float32)


def tn(a, b):
    return lax.dot_general(a, b, (((0,), (0,)), ((), ())), preferred_element_type=jnp.float32)


def nn(a, b):
    return lax.dot_general(a, b, (((1,), (0,)), ((), ())), preferred_element_type=jnp.float32)


def span_grads(q, g, rows, wk, wv):
    bf16 = jnp.bfloat16
    scale = 1.0 / math.sqrt(HD)
    heads = q.shape[1] // HD
    keys = nn(rows, wk).astype(bf16)
    values = nn(rows, wv).astype(bf16)
    cut = [slice(h * HD, (h + 1) * HD) for h in range(heads)]
    scores = jnp.concatenate([nt(q[:, s], keys[:, s]) for s in cut], axis=0) * scale
    d_weights = jnp.concatenate([nt(g[:, s], values[:, s]) for s in cut], axis=0)
    e = jnp.exp(scores - jnp.max(scores, axis=1, keepdims=True))
    probs = e / jnp.sum(e, axis=1, keepdims=True)
    row_sums = jnp.sum(d_weights * probs, axis=1, keepdims=True)
    ds = (probs * (d_weights - row_sums) * scale).astype(bf16)
    weights = probs.astype(bf16)
    attended, d_query, d_keys, d_values = [], [], [], []
    for h, s in enumerate(cut):
        w_h = weights[h * SPAN : (h + 1) * SPAN]
        ds_h = ds[h * SPAN : (h + 1) * SPAN]
        attended.append(nn(w_h, values[:, s]).astype(bf16))
        d_query.append(nn(ds_h, keys[:, s]).astype(bf16))
        d_keys.append(tn(ds_h, q[:, s]).astype(bf16))
        d_values.append(tn(w_h, g[:, s]).astype(bf16))
    dn = nt(jnp.concatenate(d_keys, axis=1), wk) + nt(jnp.concatenate(d_values, axis=1), wv)
    return (
        jnp.concatenate(attended, axis=1),
        jnp.concatenate(d_query, axis=1),
        dn.astype(bf16),
    )


def fused_kernel(
    n_dp, n_tp, treedef, owners, slots, table, queries, cotangent, key_weight, value_weight, att, dq, dt, *flat
):
    b = types.SimpleNamespace(**jax.tree_util.tree_unflatten(treedef, flat))
    bf16 = jnp.bfloat16
    me = lax.axis_index("dp")
    t = lax.axis_index("tensor")
    z, y = lax.div(me, N_Y), lax.rem(me, N_Y)
    x, core = lax.div(t, 2), lax.rem(t, 2)
    mate = x * 2 + 1 - core
    x_up, x_far, x_down = [lax.rem(x + i, N_X) for i in range(1, N_X)]
    n_req, ts, enc = b.sel.shape
    spans = n_req // 2
    wave_spans = spans // WAVES
    side = n_req // WAVES
    n_tokens = ts * n_tp
    chunks = lane_chunks(enc)
    nk = len(chunks)

    def up(d):
        return lax.rem(z + d, N_Z)

    def send_to(src, dst, ss, rs, dp_to, t_to):
        return pltpu.make_async_remote_copy(
            src_ref=src, dst_ref=dst, send_sem=ss, recv_sem=rs, device_id=(dp_to, t_to), device_id_type=MESH
        )

    def landed_all(ref, sem):
        pltpu.make_async_copy(ref, ref, sem).wait()

    loads = [
        pltpu.make_async_copy(table.at[:, pl.ds(t * ts, ts), :], b.share, b.load_sem.at[0]),
        pltpu.make_async_copy(key_weight, b.wk, b.load_sem.at[1]),
        pltpu.make_async_copy(value_weight, b.wv, b.load_sem.at[2]),
        pltpu.make_async_copy(queries, b.q, b.load_sem.at[3]),
        pltpu.make_async_copy(cotangent, b.g, b.load_sem.at[4]),
    ]
    for load in loads:
        load.start()

    barrier = pltpu.get_barrier_semaphore()
    def hello(i, carry):
        pl.semaphore_signal(
            barrier, inc=1, device_id=(lax.rem(me + i, n_dp), t), device_id_type=MESH
        )
        return carry

    lax.fori_loop(1, n_dp, hello, 0)
    for peer_t in (x_up * 2 + core, x_down * 2 + core, mate):
        pl.semaphore_signal(barrier, inc=1, device_id=(me, peer_t), device_id_type=MESH)

    lane = lax.broadcasted_iota(jnp.int32, (1, LANES), 1)
    lane_dp = lane & (n_dp - 1)
    lane_place = lax.shift_right_logical(lane, int(math.log2(n_dp))) & 1
    is_slot = lane < 2 * n_dp
    own = [owners[r % 2, r // 2] for r in range(n_req)]
    far = [lax.rem(z - lax.div(own[r], N_Y) + N_Z, N_Z) for r in range(n_req)]
    asked_row = jnp.full((1, LANES), -1, jnp.int32)
    list_row = jnp.zeros((1, LANES), jnp.int32)
    seen = jnp.zeros((1, LANES), jnp.int32)
    ranks = []
    for wave in range(WAVES):
        members = range(wave * side, (wave + 1) * side)
        taken = jnp.int32(0)
        down, dist = {}, {}
        for r in members:
            opposite = jnp.where(far[r] == HOPS, 1, 0)
            over = opposite * jnp.where(taken >= FAR_SLOTS, 1, 0)
            down[r] = jnp.where(far[r] > HOPS, 1, over)
            dist[r] = jnp.where(down[r] == 1, N_Z - far[r], far[r])
            taken = taken + opposite
        for r in members:
            slot = down[r] * side
            before = jnp.int32(0)
            for other in range(r):
                before = before + jnp.where(own[other] == own[r], 1, 0)
            for other in members:
                if other != r:
                    ahead = (dist[other] >= dist[r]) if other < r else (dist[other] > dist[r])
                    slot = slot + jnp.where(down[other] == down[r], 1, 0) * jnp.where(ahead, 1, 0)
            ranks.append(slot)
            hit = lane_dp == own[r]
            asked_row = jnp.where(
                hit & (seen == lane_place),
                jnp.where(is_slot, slots[r % 2, r // 2], wave * 2 * side + slot),
                asked_row,
            )
            seen = seen + hit.astype(jnp.int32)
            list_row = jnp.where(lane == wave * 2 * side + slot, 2 * own[r] + before, list_row)
            list_row = jnp.where(lane == (WAVES + wave) * 2 * side + slot, r, list_row)
    my_rows = jnp.concatenate([asked_row, list_row], axis=0)
    b.row[...] = my_rows

    pl.semaphore_wait(barrier, n_dp - 1 + 3)

    met, met_s = b.met, b.met_s

    def ask(i, carry):
        send_to(
            b.row, met.at[me], b.meta_send, b.meta_recv, lax.rem(me + i, n_dp), t
        ).start()
        return carry

    lax.fori_loop(1, n_dp, ask, 0)
    met[me] = my_rows
    others = met.at[pl.ds(0, n_dp - 1)]
    landed_all(others, b.meta_recv)
    to_smem = pltpu.make_async_copy(met, met_s, b.load_sem.at[5])
    loads[0].wait()
    to_smem.start()
    to_smem.wait()

    share = b.share

    def y_copy(k, g, i, from_y):
        return send_to(
            b.y_out[k][g].at[i - 1],
            b.cand[k][g].at[from_y],
            b.y_send.at[k, g],
            b.y_recv.at[k, g],
            z * N_Y + lax.rem(y + i, N_Y),
            t,
        )

    def y_pieces(k, g, to_y):
        lo, w = chunks[k]
        for n, d in enumerate(FWD_GROUPS[g]):
            for c in range(2):
                index = jnp.maximum(met_s[up(d) * N_Y + to_y, 0, c * n_dp + me], 0)
                yield n, c, share[index, :, lo : lo + w]

    def y_build(k, g):
        for i in range(1, N_Y):
            for n, c, piece in y_pieces(k, g, lax.rem(y + i, N_Y)):
                b.y_out[k][g][i - 1, n, c] = piece
            y_copy(k, g, i, y).start()
        for n, c, piece in y_pieces(k, g, y):
            b.cand[k][g][y, n, c] = piece

    def ring_rows(s, lower, forward):
        hop = HOPS + 1 - s if forward else s
        return pl.ds(0 if lower else side, FAR_SLOTS if hop == HOPS else side)

    def ring_slot(forward, wave, k, s):
        if forward:
            return b.first[wave][k] if s == 0 else b.ring[wave][k][s - 1]
        return b.lists[k].at[wave] if s == 0 else b.back[k][s - 1].at[wave]

    def ring_copy(forward, wave, k, s, up_way):
        ss, rs = (
            (b.ring_send, b.ring_recv) if forward else (b.back_send, b.back_recv)
        )
        rows = ring_rows(s, up_way if forward else not up_way, forward)
        return send_to(
            ring_slot(forward, wave, k, s - 1).at[rows],
            ring_slot(forward, wave, k, s).at[rows],
            ss.at[wave, k, 0 if up_way else 1],
            rs.at[wave, k, s - 1],
            up(1 if up_way else N_Z - 1) * N_Y + y,
            t,
        )

    def ring_step(forward, wave, k, s):
        for up_way in (True, False):
            if s > 1:
                ring_copy(forward, wave, k, s - 1, up_way).wait_send()
            ring_copy(forward, wave, k, s, up_way).start()

    def ring_landed(forward, wave, k, s):
        rs = b.ring_recv if forward else b.back_recv
        hop = HOPS + 1 - s if forward else s
        rows = pl.ds(0, 2 * (FAR_SLOTS if hop == HOPS else side))
        landed_all(ring_slot(forward, wave, k, s).at[rows], rs.at[wave, k, s - 1])

    def merge(wave, k, buf, dist):
        for down in range(2):
            d = (N_Z - dist) % N_Z if down else dist
            g, n = find_group(FWD_GROUPS, d)
            cand = b.cand[k][g]
            asker = up(d) * N_Y + y

            def one(j, carry, fresh, down=down, cand=cand, asker=asker, n=n):
                slot = down * side + j
                code = met_s[asker, 1, wave * 2 * side + slot]
                mine = cand[lax.shift_right_logical(code, 1) & (N_Y - 1), n, code & 1]
                if not fresh:
                    here = lax.div(code, 2 * N_Y) == z
                    mine = jnp.where(here, mine, buf[slot])
                buf[slot] = mine
                return carry

            if dist == HOPS:
                lax.fori_loop(0, FAR_SLOTS, functools.partial(one, fresh=True), 0)
            elif dist == HOPS - 1:
                lax.fori_loop(0, FAR_SLOTS, functools.partial(one, fresh=False), 0)
                lax.fori_loop(FAR_SLOTS, side, functools.partial(one, fresh=True), 0)
            else:
                lax.fori_loop(0, side, functools.partial(one, fresh=False), 0)

    def share_of(owner_t, row, n):
        return b.nb.at[pl.ds(row, n), pl.ds(owner_t * ts, ts)]

    def gather_start(c, lo, w):
        own_rows = b.sel.at[pl.ds(2 * c, 2), :, pl.ds(lo, w)]
        there = b.nb.at[pl.ds(2 * c, 2), pl.ds(t * ts, ts), pl.ds(lo, w)]
        for to_x in (x_up, x_down):
            send_to(
                own_rows, there, b.gx_send.at[c], b.gx_recv.at[c], me, to_x * 2 + core
            ).start()
        send_to(own_rows, there, b.gm_send.at[c], b.gm_recv.at[c], me, mate).start()

    def gather_pass(c):
        landed_all(b.nb.at[pl.ds(2 * c, 2), pl.ds(0, 2 * ts)], b.gx_recv.at[c])
        for from_x, to_x, way in ((x_down, x_up, 0), (x_up, x_down, 1)):
            one = share_of(from_x * 2 + core, 2 * c + way, 1)
            send_to(
                one, one, b.gf_send.at[c], b.gf_recv.at[c], me, to_x * 2 + core
            ).start()
        for from_x in (x_down, x_up):
            near = share_of(from_x * 2 + core, 2 * c, 2)
            send_to(near, near, b.gm_send.at[c], b.gm_recv.at[c], me, mate).start()

    def gather_far(c):
        far_share = share_of(x_far * 2 + core, 2 * c, 2)
        landed_all(far_share, b.gf_recv.at[c])
        send_to(far_share, far_share, b.gm_send.at[c], b.gm_recv.at[c], me, mate).start()

    def gather_arrived(c):
        landed_all(
            b.nb.at[pl.ds(2 * c, 2), pl.ds(0, N_X * ts)], b.gm_recv.at[c]
        )

    def gather_sent(c):
        landed_all(b.nb.at[pl.ds(2 * c, 2), pl.ds(0, 2 * ts)], b.gx_send.at[c])
        landed_all(b.sel.at[pl.ds(2 * c, 2)], b.gf_send.at[c])
        landed_all(b.nb.at[pl.ds(2 * c, 2), pl.ds(0, N_X * ts)], b.gm_send.at[c])

    needs = [(k, g) for g in range(len(FWD_GROUPS)) for k in range(nk)]
    built, landed = [0], []

    def fetch_step(wave, k, s):
        dist = HOPS + 1 - s
        g = find_group(FWD_GROUPS, dist)[0]
        while built[0] < len(needs) and built[0] <= needs.index((k, g)) + AHEAD:
            y_build(*needs[built[0]])
            built[0] += 1
        if s > 1:
            ring_landed(True, wave, k, s - 1)
        if (k, g) not in landed:
            landed_all(b.cand[k][g].at[pl.ds(0, N_Y - 1)], b.y_recv.at[k, g])
            landed.append((k, g))
        buf = ring_slot(True, wave, k, s - 1)
        merge(wave, k, buf, dist)
        if s <= HOPS:
            ring_step(True, wave, k, s)
            return
        lo, w = chunks[k]
        for r in range(wave * side, (wave + 1) * side):
            b.sel[r, :, lo : lo + w] = buf[ranks[r]]
        for c in range(wave * wave_spans, (wave + 1) * wave_spans):
            gather_start(c, lo, w)
        if k == nk - 1:
            rows = pl.ds(wave * side, side)
            b.nb[rows, pl.ds(pl.multiple_of(t * ts, ts), ts), :] = b.sel[rows]

    back_order = [d for members in BWD_GROUPS for d in members]

    def build_place():
        per = LANES // ts
        lane_tok = lax.rem(lane, ts)
        lane_piece = lax.div(lane, ts)
        tall = lax.broadcasted_iota(jnp.int32, (b.place.shape[0], LANES), 0)
        for group in range(b.place.shape[1] // LANES):
            line = jnp.full((1, LANES), -1, jnp.int32)
            for j in range(per):
                piece = group * per + j
                c, pos, from_y = piece % 2, piece // 2 % N_Z, piece // 2 // N_Z
                slab = met_s[up(back_order[pos]) * N_Y + from_y, 0, c * n_dp + me]
                line = jnp.where(lane_piece == j, slab * ts + lane_tok, line)
            b.place[:, group * LANES : (group + 1) * LANES] = jnp.where(
                tall == line, 1.0, 0.0
            ).astype(bf16)

    def mate_copy(c):
        rows = pl.ds(2 * c, 2)
        return send_to(
            b.dn.at[1 - core, :, rows],
            b.from_mate.at[:, rows],
            b.rm_send.at[c],
            b.rm_recv.at[c],
            me,
            mate,
        )

    def rows_to(to_x, src, dst, ss, rs):
        return send_to(src, dst, ss, rs, me, to_x * 2 + core)

    def far_copy(c, way):
        row = pl.ds(2 * c + way, 1)
        return rows_to(
            x_down if way else x_up,
            b.chip.at[x_far, row],
            b.from_far.at[way, pl.ds(c, 1)],
            b.rf_send.at[c],
            b.rf_recv.at[c],
        )

    def near_copy(c, way):
        rows = pl.ds(2 * c, 2)
        to_x = x_down if way else x_up
        return rows_to(
            to_x,
            b.chip.at[to_x, rows],
            b.from_near.at[way, rows],
            b.rn_send.at[c],
            b.rn_recv.at[c],
        )

    def pair_sum(c):
        mate_copy(c).wait_recv()
        rows = pl.ds(2 * c, 2)
        both = b.dn[core, :, rows].astype(jnp.float32) + b.from_mate[:, rows].astype(jnp.float32)
        b.chip[:, rows] = both.astype(bf16)
        for way in range(2):
            far_copy(c, way).start()

    def near_sum(c):
        landed_all(b.from_far.at[:, pl.ds(c, 1)], b.rf_recv.at[c])
        for way in range(2):
            to_x, row = x_down if way else x_up, 2 * c + way
            both = b.chip[to_x, row].astype(jnp.float32) + b.from_far[way, c].astype(jnp.float32)
            b.chip[to_x, row] = both.astype(bf16)
            near_copy(c, way).start()

    def last_sum(c):
        rows = pl.ds(2 * c, 2)
        total = b.chip[x, rows].astype(jnp.float32)
        landed_all(b.from_near.at[:, rows], b.rn_recv.at[c])
        for way in range(2):
            total = total + b.from_near[way, rows].astype(jnp.float32)
        wave = c // wave_spans
        b.total[wave][pl.ds(2 * c - wave * side, 2)] = total.astype(bf16)

    def attend(c):
        gather_arrived(c)
        tokens = pl.ds(c * SPAN, SPAN)
        rows = b.nb[pl.ds(2 * c, 2)].reshape(2 * n_tokens, enc)
        att_c, dq_c, dn_c = span_grads(
            b.q[tokens, :], b.g[tokens, :], rows, b.wk[...], b.wv[...]
        )
        b.att_v[tokens, :] = att_c
        b.dq_v[tokens, :] = dq_c
        for rr in range(2):
            for to_t in range(n_tp):
                lo = rr * n_tokens + to_t * ts
                b.dn[to_t % 2, to_t // 2, 2 * c + rr] = dn_c[lo : lo + ts]
        mate_copy(c).start()

    def back_lists(wave):
        for k, (lo, w) in enumerate(chunks):
            for j in range(2 * side):
                r = met_s[me, 1, (WAVES + wave) * 2 * side + j]
                b.lists[k][wave, j] = b.total[wave][jnp.maximum(r - wave * side, 0), :, lo : lo + w]

    def back_step(wave, k, s):
        if s > 1:
            ring_landed(False, wave, k, s - 1)
        if s <= HOPS:
            ring_step(False, wave, k, s)
        if wave == WAVES - 1 and s > 1:
            yb_build(k, s - 2)

    def yb_copy(k, h, i, from_y):
        at = sum(len(m) for m in BWD_GROUPS[:h])
        return send_to(
            b.yb_out[k][h].at[i - 1],
            b.got[k].at[from_y, pl.ds(at, len(BWD_GROUPS[h]))],
            b.yb_send.at[k, h],
            b.yb_recv.at[k, h],
            z * N_Y + lax.rem(y + i, N_Y),
            t,
        )

    def yb_pieces(k, h, to_y):
        for n, d in enumerate(BWD_GROUPS[h]):
            for c in range(2):
                j = met_s[up(d) * N_Y + y, 0, (2 + c) * n_dp + z * N_Y + to_y]
                j = jnp.maximum(j, 0)
                wave, slot = lax.div(j, 2 * side), lax.rem(j, 2 * side)
                if d == 0:
                    piece = b.lists[k][wave, slot]
                else:
                    piece = b.back[k][min(d, N_Z - d) - 1][wave, slot]
                yield n, c, piece

    def yb_build(k, h):
        at = sum(len(m) for m in BWD_GROUPS[:h])
        for i in range(1, N_Y):
            for n, c, piece in yb_pieces(k, h, lax.rem(y + i, N_Y)):
                b.yb_out[k][h][i - 1, n, c] = piece
            yb_copy(k, h, i, y).start()
        for n, c, piece in yb_pieces(k, h, y):
            b.got[k][y, at + n, c] = piece

    stores = [
        pltpu.make_async_copy(b.att_v, att, b.load_sem.at[6]),
        pltpu.make_async_copy(b.dq_v, dq, b.load_sem.at[7]),
    ]

    def prepare():
        build_place()
        for load in loads[1:]:
            load.wait()

    def store_all():
        for store in stores:
            store.start()

    def ring_job(step, reverse):
        def job(wave, s):
            for k in reversed(range(nk)) if reverse else range(nk):
                step(wave, k, s)

        return job

    fetch_job, back_job = ring_job(fetch_step, False), ring_job(back_step, True)
    order = (
        (fetch_job, 0, 1),
        (fetch_job, 0, 2),
        (fetch_job, 0, 3),
        (fetch_job, 1, 1),
        (fetch_job, 0, 4),
        (prepare,),
        (fetch_job, 0, 5),
        (fetch_job, 1, 2),
        (gather_pass, 0),
        (fetch_job, 1, 3),
        (gather_far, 0),
        (gather_pass, 1),
        (attend, 0),
        (gather_far, 1),
        (gather_pass, 2),
        (fetch_job, 1, 4),
        (attend, 1),
        (pair_sum, 0),
        (gather_far, 2),
        (gather_pass, 3),
        (attend, 2),
        (pair_sum, 1),
        (near_sum, 0),
        (gather_far, 3),
        (fetch_job, 1, 5),
        (attend, 3),
        (pair_sum, 2),
        (near_sum, 1),
        (last_sum, 0),
        (gather_pass, 4),
        (pair_sum, 3),
        (near_sum, 2),
        (last_sum, 1),
        (gather_far, 4),
        (gather_pass, 5),
        (near_sum, 3),
        (last_sum, 2),
        (attend, 4),
        (last_sum, 3),
        (back_lists, 0),
        (back_job, 0, 1),
        (pair_sum, 4),
        (gather_far, 5),
        (gather_pass, 6),
        (attend, 5),
        (back_job, 0, 2),
        (pair_sum, 5),
        (near_sum, 4),
        (gather_far, 6),
        (gather_pass, 7),
        (attend, 6),
        (back_job, 0, 3),
        (pair_sum, 6),
        (near_sum, 5),
        (last_sum, 4),
        (gather_far, 7),
        (attend, 7),
        (store_all,),
        (back_job, 0, 4),
        (pair_sum, 7),
        (near_sum, 6),
        (last_sum, 5),
        (near_sum, 7),
        (last_sum, 6),
        (last_sum, 7),
        (back_lists, 1),
        (back_job, 1, 1),
        (back_job, 0, 5),
        (back_job, 1, 2),
        (back_job, 1, 3),
        (back_job, 1, 4),
        (back_job, 1, 5),
    )
    for job, *numbers in order:
        job(*numbers)

    for k, (lo, w) in enumerate(chunks):
        at = 0
        for h, members in enumerate(BWD_GROUPS):
            landed_all(
                b.got[k].at[pl.ds(0, N_Y - 1), pl.ds(at, len(members))], b.yb_recv.at[k, h]
            )
            at += len(members)
        pieces = b.got[k][...].reshape(b.place.shape[1], w)
        dt[:, :, lo : lo + w] = nn(b.place[...], pieces).reshape(dt.shape[0], ts, w)

    for store in stores:
        store.wait()
    landed_all(others, b.meta_send)
    for k in range(nk):
        for g in range(len(FWD_GROUPS)):
            landed_all(b.y_out[k][g], b.y_send.at[k, g])
            landed_all(b.yb_out[k][g], b.yb_send.at[k, g])
        for wave in range(WAVES):
            for up_way in (True, False):
                ring_copy(True, wave, k, HOPS, up_way).wait_send()
                ring_copy(False, wave, k, HOPS, up_way).wait_send()

    def drain(c, carry):
        gather_sent(c)
        mate_copy(c).wait_send()
        landed_all(b.from_far.at[:, pl.ds(c, 1)], b.rf_send.at[c])
        landed_all(b.from_near.at[:, pl.ds(2 * c, 2)], b.rn_send.at[c])
        return carry

    lax.fori_loop(0, spans, drain, 0)


def finish_kernel(att_in, dq_in, dt_in, att, dq, dt):
    att[...] = att_in[...]
    dq[...] = dq_in[...]
    dt[...] = dt_in[...]


def finish(*arrays):
    parts = 4

    def spec(a):
        block = (a.shape[0] // parts, *a.shape[1:])
        return pl.BlockSpec(block, lambda i: (i,) + (0,) * (len(block) - 1))

    return pl.pallas_call(
        finish_kernel,
        grid=(parts,),
        out_shape=[jax.ShapeDtypeStruct(a.shape, a.dtype) for a in arrays],
        in_specs=[spec(a) for a in arrays],
        out_specs=[spec(a) for a in arrays],
        name="finish",
    )(*arrays)


def on_device(queries, cotangent, table, key_weight, value_weight, owners, slots):
    n_dp = lax.axis_size("dp")
    n_tp = lax.axis_size("tensor")
    n_slabs, n_tokens, enc = table.shape
    ts = n_tokens // n_tp
    spans = owners.shape[0]
    n_req = 2 * spans
    n_x = n_tp // 2
    chunks = lane_chunks(enc)
    nk = len(chunks)
    dma = pltpu.SemaphoreType.DMA
    bf16 = jnp.bfloat16
    vm = lambda *shape: pltpu.VMEM(shape, bf16)
    ng = len(FWD_GROUPS)
    side = n_req // WAVES
    scratch = dict(
        share=vm(n_slabs, ts, enc),
        wk=vm(*key_weight.shape),
        wv=vm(*value_weight.shape),
        q=vm(*queries.shape),
        g=vm(*cotangent.shape),
        att_v=vm(*queries.shape),
        dq_v=vm(*queries.shape),
        row=pltpu.VMEM((2, LANES), jnp.int32),
        met=pltpu.VMEM((n_dp, 2, LANES), jnp.int32),
        met_s=pltpu.SMEM((n_dp, 2, LANES), jnp.int32),
        y_out=[[vm(N_Y - 1, len(m), 2, ts, w) for m in FWD_GROUPS] for _, w in chunks],
        cand=[[vm(N_Y, len(m), 2, ts, w) for m in FWD_GROUPS] for _, w in chunks],
        first=[[vm(2 * side, ts, w) for _, w in chunks] for _ in range(WAVES)],
        ring=[
            [[vm(2 * side, ts, w) for _ in range(HOPS)] for _, w in chunks] for _ in range(WAVES)
        ],
        sel=vm(n_req, ts, enc),
        nb=vm(n_req, n_tokens, enc),
        place=vm(n_slabs * ts, 2 * n_dp * ts),
        dn=vm(2, n_x, n_req, ts, enc),
        from_mate=vm(n_x, n_req, ts, enc),
        chip=vm(n_x, n_req, ts, enc),
        from_far=vm(2, spans, ts, enc),
        from_near=vm(2, n_req, ts, enc),
        total=[vm(side, ts, enc) for _ in range(WAVES)],
        lists=[vm(WAVES, 2 * side, ts, w) for _, w in chunks],
        back=[[vm(WAVES, 2 * side, ts, w) for _ in range(HOPS)] for _, w in chunks],
        yb_out=[[vm(N_Y - 1, len(m), 2, ts, w) for m in BWD_GROUPS] for _, w in chunks],
        got=[vm(N_Y, N_Z, 2, ts, w) for _, w in chunks],
        load_sem=dma((8,)),
        meta_send=dma,
        meta_recv=dma,
        y_send=dma((nk, ng)),
        y_recv=dma((nk, ng)),
        yb_send=dma((nk, ng)),
        yb_recv=dma((nk, ng)),
        ring_send=dma((WAVES, nk, 2)),
        ring_recv=dma((WAVES, nk, HOPS)),
        back_send=dma((WAVES, nk, 2)),
        back_recv=dma((WAVES, nk, HOPS)),
        gx_send=dma((spans,)),
        gx_recv=dma((spans,)),
        gf_send=dma((spans,)),
        gf_recv=dma((spans,)),
        gm_send=dma((spans,)),
        gm_recv=dma((spans,)),
        rm_send=dma((spans,)),
        rm_recv=dma((spans,)),
        rf_send=dma((spans,)),
        rf_recv=dma((spans,)),
        rn_send=dma((spans,)),
        rn_recv=dma((spans,)),
    )
    leaves, treedef = jax.tree_util.tree_flatten(scratch)
    anywhere = pl.BlockSpec(memory_space=pl.ANY)
    results = pl.pallas_call(
        functools.partial(fused_kernel, n_dp, n_tp, treedef),
        out_shape=[
            jax.ShapeDtypeStruct(queries.shape, bf16),
            jax.ShapeDtypeStruct(queries.shape, bf16),
            jax.ShapeDtypeStruct((n_slabs, ts, enc), jnp.float32),
        ],
        in_specs=[pl.BlockSpec(memory_space=pltpu.SMEM)] * 2 + [anywhere] * 5,
        out_specs=[anywhere, anywhere, pl.BlockSpec(memory_space=pltpu.VMEM)],
        scratch_shapes=leaves,
        compiler_params=pltpu.CompilerParams(
            collective_id=0, has_side_effects=True, vmem_limit_bytes=VMEM_LIMIT
        ),
        name="spanned",
    )(owners.T, slots.T, table, queries, cotangent, key_weight, value_weight)
    return finish(*results)


def solution(mesh):
    in_specs = (
        P("dp", "tensor"),
        P("dp", "tensor"),
        P("dp", None, None),
        P(None, "tensor"),
        P(None, "tensor"),
        P("dp", None),
        P("dp", None),
    )
    out_specs = (P("dp", "tensor"), P("dp", "tensor"), P("dp", "tensor", None))
    return jax.shard_map(
        on_device, mesh=mesh, in_specs=in_specs, out_specs=out_specs, check_vma=False
    )
```

time: 141 us -> 137 us (0.972)
  Pallas kernels: 140 us -> 136 us
    pallas_call x1, Pallas kernels: 136 us -> 132 us  [on_device(): pl.pallas_call(functools.partial(fused_kernel, n_dp, n_tp, treedef), out_...]
where the time goes in v4:
time: 137 us
  Pallas kernels  136 us (99%)
    pallas_call x1, Pallas kernels, on_device(): pl.pallas_call(functools.partial(fused_kernel, n_dp, n_tp, treedef), out_...  132 us
    pallas_call x1, Pallas kernels, finish(): pl.pallas_call(finish_kernel, grid=(parts,), out_shape=[jax.ShapeDtypeStr...  3.77 us

profile of v4, /device:TPU:6, one launch (start us, length us, event | category | flops | bytes accessed | tf_op | source)
XLA Modules:
  0.0 136.7 jit_solution(354993472358659149)
XLA Ops:
  0.6 132.3 %spanned.1 = (bf16[512,512]{1,0:T(8,128)(2,1)}, bf16[512,512]{1,0:T(8,128)(2,1)}, f32[16,16,896]{2,1,0:T(8,128)}) custom-call(s32[2,8]{1,0:T(2,128)} %bitcast.2, s32[2,8]{1,0:T(2,128)} %bitcast.3, bf16[16,128,896]{2,1,0:T(8,128)(2,1)} %table.1, bf16[512,512]{1,0:T(8,128)(2,1)} %queries.1, bf16[512,512]{1,0:T(8,128)(2,1)} %cotangent.1, ...), custom_call_target="tpu_custom_call" | custom-call | tf_op jit(solution)/shard_map/spanned/pallas_call | solution.py:718
  132.9 3.8 %finish.1 = (bf16[512,512]{1,0:T(8,128)(2,1)}, bf16[512,512]{1,0:T(8,128)(2,1)}, f32[16,16,896]{2,1,0:T(8,128)}) custom-call(bf16[512,512]{1,0:T(8,128)(2,1)} %get-tuple-element.6.att_in, bf16[512,512]{1,0:T(8,128)(2,1)} %get-tuple-element.7.dq_in, f32[16,16,896]{2,1,0:T(8,128)} %get-tuple-element.8.dt_in), custom_call_target="tpu_custom_call" | custom-call | tf_op jit(solution)/shard_map/finish/pallas_call | solution.py:637
